TPU v7x, 32 devices: a whole 2x2x4 slice. The times are simulated.
32 devices in a mesh: head: 4 (over y, core), ctx: 8 (over z, x).
Axes of the slice: x: 2, y: 2, z: 4, core: 2. Of those that a mesh axis runs over, the one named last changes fastest.
Arguments:
- query_matrix: bfloat16 [4096, 4096], P(('ctx', 'head')), may hold values from -6 to 6
- key_matrix: bfloat16 [4096, 2048], P(('ctx', 'head')), may hold values from -6 to 6
- value_matrix: bfloat16 [4096, 2048], P(('ctx', 'head')), may hold values from -6 to 6
- documents: int32 [4096], replicated, may hold values from 0 to 6, as said below
- readers: int32 [8, 4], replicated, may hold values from 0 to 1, as said below
Outputs:
- attended: bfloat16 [4096, 4096], P(('ctx', 'head'))
Inputs may be any that keep to these rules, and one draw needn't show every extreme that they name: `documents`: starts at 0 and never falls from one token to the next; it rises by one exactly twice inside every key block other than key blocks 0 to 3 and 0 to 4, and nowhere else. `readers`: every entry of column 0 is 1. Row 0 and rows 0 to 4 are all 1.
All inputs are finite; a program needn't handle non-finite values.
Results may differ from a plain program's by a relative error of at most 0.0038.
Values may be sent and summed in bfloat16 or wider, within the bound.
No kernel may reach another device: no remote copies, remote signals or barrier semaphores. Data moves between devices by JAX's collectives and lax.ppermute only.
A program may use at most 192 MiB of HBM per device.

v0:
```python
from functools import partial

import jax
import jax.numpy as jnp
from jax import lax
from jax.sharding import PartitionSpec as P

QUERY_HEADS = 32
KEY_VALUE_HEADS = 16
HEAD_WIDTH = 128


score_scale = 168.0 ** (-0.5)
neg_large = -1e30


def passed_along(value, axis, steps):
    count = lax.axis_size(axis)
    leading, last = (max(0, -steps), min(count, count - steps))
    return lax.ppermute(value, axis, [(source, source + steps) for source in range(leading, last)])


def attend_block(running, grouped, block, query_docs, query_pos, key_docs, key_pos, allowed):
    maxima, totals, accumulated = running
    heads_local = block.shape[1] // (2 * HEAD_WIDTH)
    key_part = block[:, : heads_local * HEAD_WIDTH].reshape(block.shape[0], heads_local, HEAD_WIDTH)
    value_part = block[:, heads_local * HEAD_WIDTH :].reshape(
        block.shape[0], heads_local, HEAD_WIDTH
    )
    scores = (
        jnp.einsum("qgmd,kgd->qgmk", grouped, key_part, preferred_element_type=jnp.float32)
        * score_scale
    )
    visible = (
        (query_docs[:, None] == key_docs[None, :])
        & (key_pos[None, :] <= query_pos[:, None])
        & allowed
    )
    visible = visible[:, None, None, :]
    scores = jnp.where(visible, scores, neg_large)
    new_max = jnp.maximum(maxima, jnp.max(scores, axis=3))
    weights = jnp.where(visible, jnp.exp(scores - new_max[..., None]), 0.0)
    rescale = jnp.exp(maxima - new_max)
    totals = totals * rescale + jnp.sum(weights, axis=3)
    product = jnp.einsum(
        "qgmk,kgd->qgmd",
        weights.astype(jnp.bfloat16),
        value_part,
        preferred_element_type=jnp.float32,
    )
    accumulated = accumulated * rescale[..., None] + product
    return (new_max, totals, accumulated)


def keep_state(running):
    return running


def per_device(query_matrix, key_matrix, value_matrix, documents, readers):
    query_local, key_local, value_local = (
        lax.all_to_all(query_matrix, "head", split_axis=1, concat_axis=0, tiled=True),
        lax.all_to_all(key_matrix, "head", split_axis=1, concat_axis=0, tiled=True),
        lax.all_to_all(value_matrix, "head", split_axis=1, concat_axis=0, tiled=True),
    )
    rows_per_block = query_local.shape[0]
    heads_local = key_local.shape[1] // HEAD_WIDTH
    query_group_width = QUERY_HEADS // KEY_VALUE_HEADS
    window = readers.shape[1]
    shard_index = lax.axis_index("ctx")
    stacked = jnp.concatenate([key_local, value_local], axis=1)
    block_list = [stacked] + [
        passed_along(stacked, "ctx", distance) for distance in range(1, window)
    ]
    query_start = shard_index * rows_per_block
    row_iota = jnp.arange(rows_per_block, dtype=jnp.int32)
    query_pos = query_start + row_iota
    query_docs = lax.dynamic_slice_in_dim(documents, query_start, rows_per_block)
    grouped = query_local.reshape(rows_per_block, heads_local, query_group_width, HEAD_WIDTH)
    running = (
        jnp.full((rows_per_block, heads_local, query_group_width), neg_large, jnp.float32),
        jnp.zeros((rows_per_block, heads_local, query_group_width), jnp.float32),
        jnp.zeros((rows_per_block, heads_local, query_group_width, HEAD_WIDTH), jnp.float32),
    )
    for distance in range(window):
        owner_block = shard_index - distance
        safe_owner = jnp.maximum(owner_block, 0)
        key_pos = owner_block * rows_per_block + row_iota
        key_docs = lax.dynamic_slice_in_dim(documents, safe_owner * rows_per_block, rows_per_block)
        allowed = (owner_block >= 0) & (readers[safe_owner, distance] > 0)
        update = partial(
            attend_block,
            grouped=grouped,
            block=block_list[distance],
            query_docs=query_docs,
            query_pos=query_pos,
            key_docs=key_docs,
            key_pos=key_pos,
            allowed=True,
        )
        running = lax.cond(allowed, update, keep_state, running)
    maxima, totals, accumulated = running
    outputs = (
        (accumulated / totals[..., None])
        .astype(jnp.bfloat16)
        .reshape(rows_per_block, heads_local * query_group_width * HEAD_WIDTH)
    )
    return lax.all_to_all(outputs, "head", split_axis=0, concat_axis=1, tiled=True)


def solution(mesh):
    placed = (
        P(("ctx", "head"), None),
        P(("ctx", "head"), None),
        P(("ctx", "head"), None),
        P(),
        P(),
    )
    return jax.shard_map(
        per_device, mesh=mesh, in_specs=placed, out_specs=P(("ctx", "head"), None), check_vma=False
    )
```

profile of v0, /device:TPU:24, one launch (start us, length us, event | category | flops | bytes accessed | tf_op | source)
XLA Modules:
  0.0 158.1 jit_solution(4335816798503776621)
XLA Ops:
  0.0 2.1 %copy.96 = bf16[128,2048]{0,1:T(8,128)(2,1)} copy(bf16[128,2048]{1,0:T(8,128)(2,1)} %param.14) | data formatting | bytes 1048576 | tf_op args[1]
  2.1 3.5 %all-to-all-start = ((bf16[128,4,512]{0,2,1:T(8,128)(2,1)}), bf16[128,4,512]{0,2,1:T(8,128)(2,1)S(1)}, u32[]{:S(2)}, u32[]{:S(2)}) async-start(bf16[128,4,512]{0,2,1:T(8,128)(2,1)} %bitcast.26), calls=%async_computation | async-start | bytes 1048576 | tf_op jit(solution)/shard_map/all_to_all | solution.py:62
  7.7 6.8 %all-to-all-done = bf16[128,4,512]{0,2,1:T(8,128)(2,1)S(1)} async-done(((bf16[128,4,512]{0,2,1:T(8,128)(2,1)}), bf16[128,4,512]{0,2,1:T(8,128)(2,1)S(1)}, u32[]{:S(2)}, u32[]{:S(2)}) %all-to-all-start) | async-done | bytes 524320 | tf_op jit(solution)/shard_map/all_to_all | solution.py:62
  14.4 3.5 %all-to-all-start.2 = ((bf16[128,4,512]{0,2,1:T(8,128)(2,1)}), bf16[128,4,512]{0,2,1:T(8,128)(2,1)S(1)}, u32[]{:S(2)}, u32[]{:S(2)}) async-start(bf16[128,4,512]{0,2,1:T(8,128)(2,1)} %bitcast.30), calls=%async_computation.2 | async-start | bytes 1048576 | tf_op jit(solution)/shard_map/all_to_all | solution.py:63
  18.1 8.6 %all-to-all-done.2 = bf16[128,4,512]{0,2,1:T(8,128)(2,1)S(1)} async-done(((bf16[128,4,512]{0,2,1:T(8,128)(2,1)}), bf16[128,4,512]{0,2,1:T(8,128)(2,1)S(1)}, u32[]{:S(2)}, u32[]{:S(2)}) %all-to-all-start.2) | async-done | bytes 524320 | tf_op jit(solution)/shard_map/all_to_all | solution.py:63
  28.2 3.4 %collective-permute-start = (bf16[512,1024]{1,0:T(8,128)(2,1)}, bf16[512,1024]{1,0:T(8,128)(2,1)}, u32[]{:S(2)}, u32[]{:S(2)}) collective-permute-start(bf16[512,1024]{1,0:T(8,128)(2,1)} %pad_maximum_fusion), channel_id=1, source_target_pairs={{0,1},{1,2},{2,3},{3,4},{4,5},{5,6},{6,7},{8,9},{9,10},{10,11},{11... | collective-permute-start | bytes 3145736 | tf_op jit(solution)/shard_map/ppermute | solution.py:20
  35.2 3.5 %all-to-all-start.1 = ((bf16[128,4,1024]{2,0,1:T(8,128)(2,1)}), bf16[128,4,1024]{2,0,1:T(8,128)(2,1)S(1)}, u32[]{:S(2)}, u32[]{:S(2)}) async-start(bf16[128,4,1024]{2,0,1:T(8,128)(2,1)} %bitcast.116), calls=%async_computation.1 | async-start | bytes 2097152 | tf_op jit(solution)/shard_map/all_to_all | solution.py:61
  42.0 11.1 %all-to-all-done.1 = bf16[128,4,1024]{2,0,1:T(8,128)(2,1)S(1)} async-done(((bf16[128,4,1024]{2,0,1:T(8,128)(2,1)}), bf16[128,4,1024]{2,0,1:T(8,128)(2,1)S(1)}, u32[]{:S(2)}, u32[]{:S(2)}) %all-to-all-start.1) | async-done | bytes 1048608 | tf_op jit(solution)/shard_map/all_to_all | solution.py:61
  53.9 15.4 %conditional.4 = (f32[512,4,2]{0,2,1:T(2,128)}, f32[512,4,2]{0,2,1:T(2,128)S(1)}, f32[512,4,2,128]{3,0,2,1:T(8,128)S(1)}) conditional(s32[]{:T(128)} %convert_element_type.32, () %tuple.38, (s32[512]{0:T(512)S(1)}, s32[512]{0:T(512)S(1)}, s32[512]{0:T(512)S(1)}, bf16[512,512]{1,0:T(8,128)(2,1)S(1)}, bf16[512,4,2,128]{3,2,1,0:T(2,128)(2,1)S(1)}, ...), branch_computations={%region_0.0_spmd, %region_1.4_spmd} | conditional | flops 1102331904 | bytes 66246708 | solution.py:100
  56.8 2.5 %copy-done = f32[4,512,512,2]{2,1,3,0:T(8,128)} copy-done((f32[4,512,512,2]{2,1,3,0:T(8,128)}, f32[4,512,512,2]{2,1,3,0:T(8,128)S(1)}, u32[]{:S(2)}) %copy-start) | copy-done | bytes 8388632 | tf_op jit(solution)/shard_map/cond
  59.4 2.7 %fusion.2 = f32[512,4,2]{0,2,1:T(2,128)S(1)} fusion(f32[4,512,512,2]{2,1,3,0:T(8,128)S(1)} %get-tuple-element.400, f32[512,4,2]{0,2,1:T(2,128)} %get-tuple-element.429, pred[512,512]{0,1:T(8,128)(4,1)S(1)} %compare_and_fusion), kind=kLoop, calls=%fused_computation.4 | loop fusion | flops 10481664 | bytes 8683520 | tf_op jit(solution)/shard_map/cond/branch_1_fun/reduce_sum | solution.py:44
  63.8 5.5 %bitcast_add_fusion = f32[512,4,2,128]{3,0,2,1:T(8,128)S(1)} fusion(f32[4,512,512,2]{2,1,3,0:T(8,128)} %copy-done, f32[512,4,2]{0,2,1:T(2,128)} %get-tuple-element.429, pred[512,512]{0,1:T(8,128)(4,1)S(1)} %compare_and_fusion, f32[512,4,2]{0,2,1:T(2,128)S(1)} %get-tuple-element.391, bf16[512,4,128,1]{2,1,0,3:T(4,128)(2,1)} %bitcast.146), kind=kOutput, calls=%fused_computation.7 | convolution fusion | flops 547880960 | bytes 11304960 | tf_op jit(solution)/shard_map/cond/branch_1_fun/qgmk,kgd->qgmd/dot_general | solution.py:45
  69.5 14.2 %conditional.6 = ((f32[512,4,2]{0,2,1:T(2,128)}, f32[512,4,2]{0,2,1:T(2,128)S(1)}, f32[512,4,2,128]{3,0,2,1:T(8,128)S(1)})) conditional(s32[]{:T(128)} %convert_element_type.30, (f32[512,4,2]{0,2,1:T(2,128)}, f32[512,4,2]{0,2,1:T(2,128)S(1)}, f32[512,4,2,128]{3,0,2,1:T(8,128)S(1)}) %get-tuple-element.448, (s32[512]{0:T(512)S(1)}, s32[]{:T(128)}, ...), branch_computations={%region_8.9_spmd, %region_9.12_spmd} | conditional | flops 1102848512 | bytes 36978784 | solution.py:100
  70.2 2.3 %copy.104 = bf16[512,1024]{0,1:T(8,128)(2,1)} copy(bf16[512,1024]{1,0:T(8,128)(2,1)} %get-tuple-element.375) | data formatting | bytes 2097152 | tf_op jit(solution)/shard_map
  73.7 2.2 %fusion.29 = (f32[512,4,2]{0,2,1:T(2,128)S(1)}, f32[4,512,512,2]{2,1,3,0:T(8,128)S(1)}) fusion(pred[512,512]{0,1:T(8,128)(4,1)S(1)} %compare_and_fusion.2, bf16[512,4,128,1]{0,2,3,1:T(8,128)(2,1)S(1)} %bitcast.143, bf16[512,4,2,128]{3,2,1,0:T(2,128)(2,1)S(1)} %get-tuple-element.376), kind=kOutput, calls=%fused_computation.37 | convolution fusion | flops 543158272 | bytes 10240000 | tf_op jit(solution)/shard_map/cond/branch_1_fun/qgmd,kgd->qgmk/dot_general | solution.py:31
  76.7 2.0 %fusion.31 = f32[512,4,2]{0,2,1:T(2,128)S(1)} fusion(f32[4,512,512,2]{2,1,3,0:T(8,128)S(1)} %get-tuple-element.408, f32[512,4,2]{0,2,1:T(2,128)S(1)} %max.17, pred[512,512]{0,1:T(8,128)(4,1)S(1)} %compare_and_fusion.2), kind=kLoop, calls=%fused_computation.39 | loop fusion | flops 10481664 | bytes 8683520 | tf_op jit(solution)/shard_map/cond/branch_1_fun/reduce_sum | solution.py:44
  80.1 3.7 %bitcast_add_fusion.2 = f32[512,4,2,128]{3,0,2,1:T(8,128)S(1)} fusion(f32[512,4,2,128]{3,0,2,1:T(8,128)S(1)} %get-tuple-element.209, bf16[512,4,128,1]{0,2,3,1:T(8,128)(2,1)S(1)} %bitcast.149, f32[4,512,512,2]{2,1,3,0:T(8,128)S(1)} %get-tuple-element.408, f32[512,4,2]{0,2,1:T(2,128)S(1)} %max.17, pred[512,512]{0,1:T(8,128)(4,1)S(1)} %compare_and_fusion.2, ...), kind=kOutput, calls=%fused_computation.42 | convolution fusion | flops 548405248 | bytes 13402112 | tf_op jit(solution)/shard_map/cond/branch_1_fun/qgmk,kgd->qgmd/dot_general | solution.py:45
  83.8 39.5 %collective-permute-done.2 = bf16[512,1024]{1,0:T(8,128)(2,1)} collective-permute-done((bf16[512,1024]{1,0:T(8,128)(2,1)}, bf16[512,1024]{1,0:T(8,128)(2,1)}, u32[]{:S(2)}, u32[]{:S(2)}) %collective-permute-start.2) | collective-permute-done | bytes 1048608 | tf_op jit(solution)/shard_map/ppermute | solution.py:20
  123.3 13.4 %conditional.7 = ((f32[512,4,2]{0,2,1:T(2,128)S(1)}, f32[512,4,2,128]{3,0,2,1:T(8,128)S(1)})) conditional(s32[]{:T(128)} %convert_element_type.29, (f32[512,4,2]{0,2,1:T(2,128)S(1)}, f32[512,4,2,128]{3,0,2,1:T(8,128)S(1)}) %tuple.42, (s32[512]{0:T(512)S(1)}, s32[]{:T(128)}, s32[4096]{0:T(1024)S(1)}, s32[]{:T(128)}, s32[512]{0:T(512)S(1)}, ...), branch_computations={%region_12.13_spmd, %region_13.16_spmd} | conditional | flops 1102848512 | bytes 36946008 | solution.py:100
  123.6 2.3 %copy.106 = bf16[512,1024]{0,1:T(8,128)(2,1)} copy(bf16[512,1024]{1,0:T(8,128)(2,1)} %get-tuple-element.386) | data formatting | bytes 2097152 | tf_op jit(solution)/shard_map
  127.2 2.2 %fusion.42 = (f32[512,4,2]{0,2,1:T(2,128)S(1)}, f32[4,512,512,2]{2,1,3,0:T(8,128)S(1)}) fusion(pred[512,512]{0,1:T(8,128)(4,1)S(1)} %compare_and_fusion.3, bf16[512,4,128,1]{0,2,3,1:T(8,128)(2,1)S(1)} %bitcast.144, bf16[512,4,2,128]{3,2,1,0:T(2,128)(2,1)S(1)} %get-tuple-element.387), kind=kOutput, calls=%fused_computation.54 | convolution fusion | flops 543158272 | bytes 10240000 | tf_op jit(solution)/shard_map/cond/branch_1_fun/qgmd,kgd->qgmk/dot_general | solution.py:31
  130.1 2.0 %fusion.44 = f32[512,4,2]{0,2,1:T(2,128)S(1)} fusion(f32[4,512,512,2]{2,1,3,0:T(8,128)S(1)} %get-tuple-element.412, f32[512,4,2]{0,2,1:T(2,128)S(1)} %max.18, pred[512,512]{0,1:T(8,128)(4,1)S(1)} %compare_and_fusion.3), kind=kLoop, calls=%fused_computation.56 | loop fusion | flops 10481664 | bytes 8683520 | tf_op jit(solution)/shard_map/cond/branch_1_fun/reduce_sum | solution.py:44
  132.9 3.7 %bitcast_add_fusion.3 = f32[512,4,2,128]{3,0,2,1:T(8,128)S(1)} fusion(f32[512,4,2,128]{3,0,2,1:T(8,128)S(1)} %get-tuple-element.220, bf16[512,4,128,1]{0,2,3,1:T(8,128)(2,1)S(1)} %bitcast.150, f32[4,512,512,2]{2,1,3,0:T(8,128)S(1)} %get-tuple-element.412, f32[512,4,2]{0,2,1:T(2,128)S(1)} %max.18, pred[512,512]{0,1:T(8,128)(4,1)S(1)} %compare_and_fusion.3, ...), kind=kOutput, calls=%fused_computation.59 | convolution fusion | flops 548405248 | bytes 13402112 | tf_op jit(solution)/shard_map/cond/branch_1_fun/qgmk,kgd->qgmd/dot_general | solution.py:45
  139.2 16.9 %all_to_all.73 = bf16[4,128,1024]{2,1,0:T(8,128)(2,1)S(1)} all-to-all(bf16[4,128,1024]{2,1,0:T(8,128)(2,1)S(1)} %all_to_all.65), channel_id=1, replica_groups=mesh['head'=4,'ctx'=8] {'head'}, dimensions={0} | all-to-all | bytes 2097152 | tf_op jit(solution)/shard_map/all_to_all | solution.py:107
  (48 shorter events, 24.9 us)
Async XLA Ops:
  0.0 34.2 %copy-start.1 = (bf16[128,4096]{1,0:T(8,128)(2,1)S(1)}, bf16[128,4096]{1,0:T(8,128)(2,1)}, u32[]{:S(2)}) copy-start(bf16[128,4096]{1,0:T(8,128)(2,1)} %param.13) | copy-start | bytes 3145732
  0.0 38.8 %copy-start.3 = (s32[8,4]{0,1:T(4,128)S(1)}, s32[8,4]{0,1:T(4,128)}, u32[]{:S(2)}) copy-start(s32[8,4]{0,1:T(4,128)} %param.17) | copy-start | bytes 388
  0.0 41.9 %copy-start.2 = (s32[4096]{0:T(1024)S(1)}, s32[4096]{0:T(1024)}, u32[]{:S(2)}) copy-start(s32[4096]{0:T(1024)} %param.16) | copy-start | bytes 49156
  2.1 12.3 %all-to-all-start = ((bf16[128,4,512]{0,2,1:T(8,128)(2,1)}), bf16[128,4,512]{0,2,1:T(8,128)(2,1)S(1)}, u32[]{:S(2)}, u32[]{:S(2)}) async-start(bf16[128,4,512]{0,2,1:T(8,128)(2,1)} %bitcast.26), calls=%async_computation | async-start | bytes 1048576 | tf_op jit(solution)/shard_map/all_to_all | solution.py:62
  14.4 12.3 %all-to-all-start.2 = ((bf16[128,4,512]{0,2,1:T(8,128)(2,1)}), bf16[128,4,512]{0,2,1:T(8,128)(2,1)S(1)}, u32[]{:S(2)}, u32[]{:S(2)}) async-start(bf16[128,4,512]{0,2,1:T(8,128)(2,1)} %bitcast.30), calls=%async_computation.2 | async-start | bytes 1048576 | tf_op jit(solution)/shard_map/all_to_all | solution.py:63
  28.2 41.2 %collective-permute-start = (bf16[512,1024]{1,0:T(8,128)(2,1)}, bf16[512,1024]{1,0:T(8,128)(2,1)}, u32[]{:S(2)}, u32[]{:S(2)}) collective-permute-start(bf16[512,1024]{1,0:T(8,128)(2,1)} %pad_maximum_fusion), channel_id=1, source_target_pairs={{0,1},{1,2},{2,3},{3,4},{4,5},{5,6},{6,7},{8,9},{9,10},{10,11},{11... | collective-permute-start | bytes 3145736 | tf_op jit(solution)/shard_map/ppermute | solution.py:20
  31.6 38.0 %collective-permute-start.1 = (bf16[512,1024]{1,0:T(8,128)(2,1)}, bf16[512,1024]{1,0:T(8,128)(2,1)}, u32[]{:S(2)}, u32[]{:S(2)}) collective-permute-start(bf16[512,1024]{1,0:T(8,128)(2,1)} %pad_maximum_fusion), channel_id=1, source_target_pairs={{0,2},{1,3},{2,4},{3,5},{4,6},{5,7},{8,10},{9,11},{10,12},{11,13},... | collective-permute-start | bytes 3145736 | tf_op jit(solution)/shard_map/ppermute | solution.py:20
  32.9 90.4 %collective-permute-start.2 = (bf16[512,1024]{1,0:T(8,128)(2,1)}, bf16[512,1024]{1,0:T(8,128)(2,1)}, u32[]{:S(2)}, u32[]{:S(2)}) collective-permute-start(bf16[512,1024]{1,0:T(8,128)(2,1)} %pad_maximum_fusion), channel_id=1, source_target_pairs={{0,3},{1,4},{2,5},{3,6},{4,7},{8,11},{9,12},{10,13},{11,14},{12,15... | collective-permute-start | bytes 3145736 | tf_op jit(solution)/shard_map/ppermute | solution.py:20
  35.2 18.0 %all-to-all-start.1 = ((bf16[128,4,1024]{2,0,1:T(8,128)(2,1)}), bf16[128,4,1024]{2,0,1:T(8,128)(2,1)S(1)}, u32[]{:S(2)}, u32[]{:S(2)}) async-start(bf16[128,4,1024]{2,0,1:T(8,128)(2,1)} %bitcast.116), calls=%async_computation.1 | async-start | bytes 2097152 | tf_op jit(solution)/shard_map/all_to_all | solution.py:61
  56.1 3.2 %copy-start = (f32[4,512,512,2]{2,1,3,0:T(8,128)}, f32[4,512,512,2]{2,1,3,0:T(8,128)S(1)}, u32[]{:S(2)}) copy-start(f32[4,512,512,2]{2,1,3,0:T(8,128)S(1)} %get-tuple-element.400) | copy-start | bytes 25165828 | tf_op jit(solution)/shard_map/cond
where the time goes:
time: 159 us; the launch traced here: 158 us
  waiting for transfers between devices  66 us (42%)
  local copies, waits for them, and re-layouts  22.4 us (14%)
  matrix products  19.1 us (12%)
  blocking collectives  16.9 us (11%)
  starting transfers between devices  16.4 us (10%)
  other arithmetic  14 us (9%)
  between operations  2.69 us (2%)
    ppermute x3, waiting for transfers between devices, passed_along(): lax.ppermute(value, axis, [(source, source + steps) for source in range(l...  39.5 us
    all_to_all x1, blocking collectives, per_device(): lax.all_to_all(outputs, 'head', split_axis=0, concat_axis=1, tiled=True)  16.9 us
    dot_general x3, matrix products, attend_block(): jnp.einsum('qgmk,kgd->qgmd', weights.astype(jnp.bfloat16), value_part, pr...  12.9 us
    all_to_all x1, waiting for transfers between devices, per_device(): lax.all_to_all(query_matrix, 'head', split_axis=1, concat_axis=0, tiled=T...  11.1 us
    all_to_all x1, waiting for transfers between devices, per_device(): lax.all_to_all(value_matrix, 'head', split_axis=1, concat_axis=0, tiled=T...  8.59 us
    reduce_sum x3, other arithmetic, attend_block(): totals = totals * rescale + jnp.sum(weights, axis=3)  6.84 us
    all_to_all x1, waiting for transfers between devices, per_device(): lax.all_to_all(key_matrix, 'head', split_axis=1, concat_axis=0, tiled=True)  6.77 us
    dot_general x3, matrix products, attend_block(): jnp.einsum('qgmd,kgd->qgmk', grouped, key_part, preferred_element_type=jn...  6.23 us
  transfers between devices with their start and end apart: 6, of which 4 were waited for; matrix products, arithmetic and copies ran while one was open for 20% of the time, Pallas kernels for 0%

commit v1 on v0

v1 whole, which is shorter than its diff:
```python
import functools
import math

import jax
import jax.numpy as jnp
from jax import lax
from jax.experimental import pallas as pl
from jax.experimental.pallas import tpu as pltpu
from jax.sharding import PartitionSpec as P

QUERY_HEADS = 32
KEY_VALUE_HEADS = 16
HEAD_WIDTH = 128
GROUP = QUERY_HEADS // KEY_VALUE_HEADS

log_scale = 168.0 ** (-0.5) * math.log2(math.e)
neg_large = -1e30
VMEM_LIMIT = 40 * 1024 * 1024


def wanted_blocks(count, window):
    middle = count // 2
    whole = set(range(window)) | set(range(max(middle - window, 0), middle + 1))
    return [
        [b for b in range(max(0, t - window + 1), t) if all(m in whole for m in range(b + 1, t))]
        for t in range(count)
    ]


def plan_rounds(count, window, kind, early):
    wanted = wanted_blocks(count, window)
    held = [{c: 0} for c in range(count)]
    rounds = []

    def missing(t):
        return [b for b in wanted[t] if b not in held[t]]

    def send(k, s, t, b):
        rounds[k][t] = (s, b, held[s][b])
        held[t][b] = k + 1

    for k in range(3):
        rounds.append({})
        had = [dict(x) for x in held]
        for s in range(count):
            t = s + 2 if (k + kind) % 2 == 0 else s ^ 1
            if t >= count:
                continue
            choice = [b for b in had[s] if b in missing(t)]
            if choice:
                send(k, s, t, max(choice))
    for t in range(count):
        for b in missing(t):
            whole_way = t - b == 1 or early
            placed = False
            if whole_way:
                for k in range(len(rounds)):
                    busy = {entry[0] for entry in rounds[k].values()}
                    if b not in busy and t not in rounds[k]:
                        send(k, b, t, b)
                        placed = True
                        break
            k = 3
            while not placed:
                if k == len(rounds):
                    rounds.append({})
                busy = {entry[0] for entry in rounds[k].values()}
                holders = [
                    s
                    for s in range(count)
                    if b in held[s] and held[s][b] <= k and s not in busy
                ]
                holders.sort(key=lambda s: (abs(t - s) != 2, abs(t - s)))
                if holders and t not in rounds[k]:
                    send(k, holders[0], t, b)
                    placed = True
                k += 1
    return rounds


def move(operands, copies, shapes, head_index):
    count_in = len(operands)

    def kernel(head_ref, *refs):
        h = head_ref[0]
        sources, targets, sems = refs[:count_in], refs[count_in:-1], refs[-1]

        def at(value):
            return pl.multiple_of(value(h), 128) if callable(value) else value

        started = []
        for number, (s, row, rows, col, cols, t, to_row, to_col) in enumerate(copies):
            copy = pltpu.make_async_copy(
                sources[s].at[pl.ds(at(row), rows), pl.ds(at(col), cols)],
                targets[t].at[pl.ds(at(to_row), rows), pl.ds(at(to_col), cols)],
                sems.at[number],
            )
            copy.start()
            started.append(copy)
        for copy in started:
            copy.wait()

    moved = sum(c[2] * c[4] * 2 for c in copies)
    return pl.pallas_call(
        kernel,
        out_shape=[jax.ShapeDtypeStruct(s, jnp.bfloat16) for s in shapes],
        grid_spec=pltpu.PrefetchScalarGridSpec(
            num_scalar_prefetch=1,
            grid=(1,),
            in_specs=[pl.BlockSpec(memory_space=pl.ANY)] * count_in,
            out_specs=[pl.BlockSpec(memory_space=pl.ANY)] * len(shapes),
            scratch_shapes=[pltpu.SemaphoreType.DMA((len(copies),))],
        ),
        cost_estimate=pl.CostEstimate(flops=0, bytes_accessed=2 * moved, transcendentals=0),
    )(head_index, *operands)


def attend(queries, chunk, blocks, with_own, state, final, meta, documents, doc_rows, readers, window):
    slots = len(queries)
    token_count = queries[0].shape[0]
    rows = slots * token_count
    kv_heads = blocks[0].shape[1] // (2 * HEAD_WIDTH)
    width = GROUP * HEAD_WIDTH
    count = len(blocks)

    def kernel(meta_ref, doc_ref, read_ref, *refs):
        refs = list(refs)
        q_refs = [refs.pop(0) for _ in range(slots)]
        kv_refs = [(refs.pop(0), refs.pop(0)) for _ in range(count)]
        rows_ref = refs.pop(0)
        if not with_own:
            acc_in, stat_in = refs.pop(0), refs.pop(0)
        if final:
            out_refs = [refs.pop(0) for _ in range(slots)]
        else:
            acc_out, stat_out = refs.pop(0), refs.pop(0)
        q_all, acc, top, total, bias = refs
        step = pl.program_id(0)
        ctx, head = meta_ref[0], meta_ref[1]

        for r in range(slots):
            q_all[r * token_count : (r + 1) * token_count, :] = q_refs[r][...]
        if not with_own:
            acc[...] = acc_in[...]
            for g in range(GROUP):
                stats = stat_in[:, g * HEAD_WIDTH : (g + 1) * HEAD_WIDTH]
                top[g] = stats[:, 0:1]
                total[g] = stats[:, HEAD_WIDTH // 2 : HEAD_WIDTH // 2 + 1]

        def make_bias(index, block, own):
            def of_queries(i, _):
                place_q = head ^ i
                here = rows_ref[pl.ds(ctx * slots + place_q, 1), :]
                q_docs = jnp.broadcast_to(here, (token_count, token_count)).T
                for j in range(slots):
                    place_k = head ^ j
                    k_docs = rows_ref[pl.ds(block * slots + place_k, 1), :]
                    seen = q_docs == k_docs
                    if own:
                        q_pos = place_q * token_count + lax.broadcasted_iota(
                            jnp.int32, (token_count, token_count), 0
                        )
                        k_pos = place_k * token_count + lax.broadcasted_iota(
                            jnp.int32, (token_count, token_count), 1
                        )
                        seen = seen & (k_pos <= q_pos)
                    bias[
                        index,
                        pl.ds(pl.multiple_of(i * token_count, token_count), token_count),
                        j * token_count : (j + 1) * token_count,
                    ] = jnp.where(seen, 0.0, neg_large)
                return 0

            lax.fori_loop(0, slots, of_queries, 0)

        def run(index, masked, first):
            k_ref, v_ref = kv_refs[index]

            def tile(i, _):
                part = pl.ds(pl.multiple_of(i * token_count, token_count), token_count)
                for g in range(GROUP):
                    lanes = slice(g * HEAD_WIDTH, (g + 1) * HEAD_WIDTH)
                    scores = lax.dot_general(
                        q_all[part, lanes],
                        k_ref[...],
                        (((1,), (1,)), ((), ())),
                        preferred_element_type=jnp.float32,
                    )
                    if masked:
                        scores = scores + bias[index, part, :]
                    peak = jnp.max(scores, axis=1, keepdims=True)
                    if not first:
                        before = top[g, part, :]
                        peak = jnp.maximum(peak, before)
                    weights = jnp.exp2((scores - peak) * log_scale)
                    product = jnp.dot(
                        weights.astype(jnp.bfloat16),
                        v_ref[...],
                        preferred_element_type=jnp.float32,
                    )
                    added = jnp.sum(weights, axis=1, keepdims=True)
                    if first:
                        total[g, part, :] = added
                        acc[part, lanes] = product
                    else:
                        fade = jnp.exp2((before - peak) * log_scale)
                        total[g, part, :] = total[g, part, :] * fade + added
                        acc[part, lanes] = acc[part, lanes] * fade + product
                    top[g, part, :] = peak
                return 0

            lax.fori_loop(0, slots, tile, 0, unroll=2)

        q_first, q_last = doc_ref[ctx * rows], doc_ref[ctx * rows + rows - 1]
        other = 0
        for index in range(count):
            if with_own and index == 0:

                @pl.when(step == 0)
                def _():
                    make_bias(0, ctx, True)

                run(0, True, True)
                continue
            number = meta_ref[2 + other]
            other += 1
            block = jnp.maximum(number, 0)
            k_first, k_last = doc_ref[block * rows], doc_ref[block * rows + rows - 1]
            distance = jnp.clip(ctx - block, 0, window - 1)
            live = (
                (number >= 0) & (read_ref[block * window + distance] > 0) & (k_last == q_first)
            )
            full = k_first == q_last

            @pl.when(live & full)
            def _(index=index):
                run(index, False, False)

            @pl.when(live & jnp.logical_not(full))
            def _(index=index, block=block):
                @pl.when(step == 0)
                def _():
                    make_bias(index, block, False)

                run(index, True, False)

        if final:
            for r in range(slots):
                part = slice(r * token_count, (r + 1) * token_count)
                for g in range(GROUP):
                    lanes = slice(g * HEAD_WIDTH, (g + 1) * HEAD_WIDTH)
                    out_refs[r][:, lanes] = (acc[part, lanes] / total[g, part, :]).astype(
                        jnp.bfloat16
                    )
        else:
            acc_out[...] = acc[...]
            low = lax.broadcasted_iota(jnp.int32, (rows, HEAD_WIDTH), 1) < HEAD_WIDTH // 2
            for g in range(GROUP):
                stat_out[:, g * HEAD_WIDTH : (g + 1) * HEAD_WIDTH] = jnp.where(
                    low, top[g], total[g]
                )

    kv_specs = []
    kv_operands = []
    for block in blocks:
        kv_specs.append(pl.BlockSpec((rows, HEAD_WIDTH), lambda i, *_: (0, i)))
        kv_specs.append(pl.BlockSpec((rows, HEAD_WIDTH), lambda i, *_: (0, i + kv_heads)))
        kv_operands += [block, block]
    wide = pl.BlockSpec((rows, width), lambda i, *_: (0, i))
    thin = pl.BlockSpec((token_count, width), lambda i, *_: (0, i))
    in_specs = [
        pl.BlockSpec((token_count, width), lambda i, *_: (0, i + chunk * kv_heads))
        for _ in range(slots)
    ]
    in_specs += kv_specs + [pl.BlockSpec(doc_rows.shape, lambda i, *_: (0, 0))]
    operands = list(queries) + kv_operands + [doc_rows]
    if not with_own:
        in_specs += [wide, wide]
        operands += list(state)
    if final:
        out_shape = [jax.ShapeDtypeStruct((token_count, kv_heads * width), jnp.bfloat16)] * slots
        out_specs = [thin] * slots
    else:
        out_shape = [jax.ShapeDtypeStruct((rows, kv_heads * width), jnp.float32)] * 2
        out_specs = [wide, wide]
    scores_made = kv_heads * GROUP * rows * rows * count
    return pl.pallas_call(
        kernel,
        out_shape=out_shape,
        grid_spec=pltpu.PrefetchScalarGridSpec(
            num_scalar_prefetch=3,
            grid=(kv_heads,),
            in_specs=in_specs,
            out_specs=out_specs,
            scratch_shapes=[
                pltpu.VMEM((rows, width), jnp.bfloat16),
                pltpu.VMEM((rows, width), jnp.float32),
                pltpu.VMEM((GROUP, rows, 1), jnp.float32),
                pltpu.VMEM((GROUP, rows, 1), jnp.float32),
                pltpu.VMEM((count, rows, rows), jnp.float32),
            ],
        ),
        compiler_params=pltpu.CompilerParams(vmem_limit_bytes=VMEM_LIMIT),
        cost_estimate=pl.CostEstimate(
            flops=4 * scores_made * HEAD_WIDTH,
            bytes_accessed=4 * rows * kv_heads * width,
            transcendentals=scores_made,
        ),
    )(meta, documents, readers, *operands)


def per_device(query_matrix, key_matrix, value_matrix, documents, readers):
    shards = lax.axis_size("ctx")
    slots = lax.axis_size("head")
    window = readers.shape[1]
    tokens = query_matrix.shape[0]
    rows = tokens * slots
    heads_local = key_matrix.shape[1] // HEAD_WIDTH // slots
    chunks = 2 if heads_local % 2 == 0 else 1
    chunk_heads = heads_local // chunks
    chunk_keys = chunk_heads * HEAD_WIDTH
    chunk_queries = chunk_keys * GROUP
    ctx, head = lax.axis_index("ctx"), lax.axis_index("head")
    head_index = head.astype(jnp.int32).reshape(1)
    doc_rows = documents.reshape(shards * slots, tokens)

    plans = []
    for chunk in range(chunks):
        kinds = [plan_rounds(shards, window, kind, chunk == chunks - 1) for kind in (0, 1)]
        length = max(len(k) for k in kinds)
        plans.append([k + [{}] * (length - len(k)) for k in kinds])
    table = [
        [
            [
                value
                for plan in plans
                for k in range(len(plan[0]))
                for value in (
                    next((e[2] for e in plan[h % 2][k].values() if e[0] == c), -1),
                    plan[h % 2][k][c][1] if c in plan[h % 2][k] else -1,
                )
            ]
            for h in range(slots)
        ]
        for c in range(shards)
    ]
    mine = lax.dynamic_slice(
        jnp.array(table, jnp.int32), (ctx, head, 0), (1, 1, len(table[0][0]))
    ).reshape(-1)

    def swap(value, r):
        return lax.ppermute(value, "head", [(h, h ^ r) for h in range(slots)])

    copies = []
    shapes = []
    for chunk in range(chunks):
        for r in range(slots):
            for source in range(2):
                copies.append(
                    (
                        source,
                        0,
                        tokens,
                        lambda h, r=r, chunk=chunk: (h ^ r) * (heads_local * HEAD_WIDTH)
                        + chunk * chunk_keys,
                        chunk_keys,
                        chunk * slots + r,
                        0,
                        source * chunk_keys,
                    )
                )
            shapes.append((tokens, 2 * chunk_keys))
    pieces = move([key_matrix, value_matrix], copies, shapes, head_index)
    own = []
    for chunk in range(chunks):
        parts = pieces[chunk * slots : (chunk + 1) * slots]
        parts = [parts[0]] + [swap(parts[r], r) for r in range(1, slots)]
        own.append(
            move(
                parts,
                [(r, 0, tokens, 0, 2 * chunk_keys, 0, r * tokens, 0) for r in range(slots)],
                [(rows, 2 * chunk_keys)],
                head_index,
            )[0]
        )
    local_queries = GROUP * heads_local * HEAD_WIDTH
    queries = move(
        [query_matrix],
        [
            (0, 0, tokens, lambda h, r=r: (h ^ r) * local_queries, local_queries, r, 0, 0)
            for r in range(slots)
        ],
        [(tokens, local_queries)] * slots,
        head_index,
    )
    queries = [queries[0]] + [swap(queries[r], r) for r in range(1, slots)]

    held = [[block] for block in own]
    numbers = [[] for _ in own]
    cursor = [sum(2 * len(plans[p][0]) for p in range(chunk)) for chunk in range(chunks)]
    for k in range(max(len(plan[0]) for plan in plans)):
        for chunk in range(chunks):
            kinds = plans[chunk]
            if k >= len(kinds[0]):
                continue
            pairs, used = [], set()
            for h in range(slots):
                for target, (source, _, slot) in kinds[h % 2][k].items():
                    pairs.append((h * shards + source, h * shards + target))
                    used.add(slot)
            used = sorted(used)
            operand = held[chunk][used[0]]
            for slot in used[1:]:
                operand = jnp.where(
                    mine[cursor[chunk] + 2 * k] == slot, held[chunk][slot], operand
                )
            numbers[chunk].append(mine[cursor[chunk] + 2 * k + 1])
            held[chunk].append(lax.ppermute(operand, ("head", "ctx"), pairs))

    results = []
    for chunk in range(chunks):
        blocks, ids = held[chunk], numbers[chunk]
        place = jnp.stack([ctx, head]).astype(jnp.int32)
        common = (documents, doc_rows, readers.reshape(-1), window)
        state = attend(
            queries, chunk, blocks[:3], True, None, False,
            jnp.concatenate([place, jnp.stack(ids[:2])]), *common,
        )
        outs = attend(
            queries, chunk, blocks[3:], False, state, True,
            jnp.concatenate([place, jnp.stack(ids[2:])]), *common,
        )
        results += [outs[0]] + [swap(outs[r], r) for r in range(1, slots)]

    return move(
        results,
        [
            (
                chunk * slots + r,
                0,
                tokens,
                0,
                chunk_queries,
                0,
                0,
                lambda h, r=r, chunk=chunk: (h ^ r) * local_queries + chunk * chunk_queries,
            )
            for chunk in range(chunks)
            for r in range(slots)
        ],
        [query_matrix.shape],
        head_index,
    )[0]


def solution(mesh):
    placed = (
        P(("ctx", "head"), None),
        P(("ctx", "head"), None),
        P(("ctx", "head"), None),
        P(),
        P(),
    )
    return jax.shard_map(
        per_device, mesh=mesh, in_specs=placed, out_specs=P(("ctx", "head"), None), check_vma=False
    )
```

time: 159 us -> 283 us (1.78)
  the two profiles are of different devices: /device:TPU:24 before, /device:TPU:21 now
where the time goes in v1:
time: 283 us; the launch traced here: 282 us
  Pallas kernels  189 us (67%)
  starting transfers between devices  43.1 us (15%)
  waiting for transfers between devices  36.8 us (13%)
  local copies, waits for them, and re-layouts  6.9 us (2%)
  other arithmetic  4.85 us (2%)
    pallas_call x5, Pallas kernels, move(): pl.pallas_call(kernel, out_shape=[jax.ShapeDtypeStruct(s, jnp.bfloat16) f...  133 us
    pallas_call x4, Pallas kernels, attend(): pl.pallas_call(kernel, out_shape=out_shape, grid_spec=pltpu.PrefetchScala...  56 us
    ppermute x15, waiting for transfers between devices, swap(): return lax.ppermute(value, 'head', [(h, h ^ r) for h in range(slots)])  24.3 us
    ppermute x15, starting transfers between devices, swap(): return lax.ppermute(value, 'head', [(h, h ^ r) for h in range(slots)])  23.4 us
    ppermute x7, starting transfers between devices, per_device(): held[chunk].append(lax.ppermute(operand, ('head', 'ctx'), pairs))  19.7 us
    ppermute x7, waiting for transfers between devices, per_device(): held[chunk].append(lax.ppermute(operand, ('head', 'ctx'), pairs))  12.5 us
  transfers between devices with their start and end apart: 22, of which 10 were waited for; matrix products, arithmetic and copies ran while one was open for 2% of the time, Pallas kernels for 38%

profile of v1, /device:TPU:21, one launch (start us, length us, event | category | flops | bytes accessed | tf_op | source)
XLA Modules:
  0.0 282.3 jit_solution(621678574256317642)
XLA Ops:
  0.0 33.0 %shard_map.65 = (bf16[128,512]{1,0:T(8,128)(2,1)}, bf16[128,512]{1,0:T(8,128)(2,1)}, bf16[128,512]{1,0:T(8,128)(2,1)}, bf16[128,512]{1,0:T(8,128)(2,1)}, bf16[12...) custom-call(s32[1]{0:T(128)} %bitcast.head_ref, ...), custom_call_target="tpu_custom_call" | custom-call | bytes 2097152 | tf_op jit(solution)/shard_map/pallas_call | solution.py:104
  35.5 3.6 %collective-permute-done.4.refs_2_ = bf16[128,512]{1,0:T(8,128)(2,1)S(1)} collective-permute-done((bf16[128,512]{1,0:T(8,128)(2,1)}, bf16[128,512]{1,0:T(8,128)(2,1)S(1)}, u32[]{:S(2)}, u32[]{:S(2)}) %collective-permute-start.4) | collective-permute-done | bytes 131104 | tf_op jit(solution)/shard_map/ppermute | solution.py:352
  39.0 3.0 %collective-permute-done.5.refs_3_ = bf16[128,512]{1,0:T(8,128)(2,1)S(1)} collective-permute-done((bf16[128,512]{1,0:T(8,128)(2,1)}, bf16[128,512]{1,0:T(8,128)(2,1)S(1)}, u32[]{:S(2)}, u32[]{:S(2)}) %collective-permute-start.5) | collective-permute-done | bytes 131104 | tf_op jit(solution)/shard_map/ppermute | solution.py:352
  42.7 17.0 %shard_map.66.refs_4_.refs_5_ = bf16[512,512]{1,0:T(8,128)(2,1)} custom-call(s32[1]{0:T(128)} %bitcast.head_ref, bf16[128,512]{1,0:T(8,128)(2,1)} %get-tuple-element.33.refs_0_, bf16[128,512]{1,0:T(8,128)(2,1)} %copy-done.18, bf16[128,512]{1,0:T(8,128)(2,1)} %copy-done.19, bf16[128,512]{1,0:T(8,128)(2,1)} %copy-done.20), custom_call_target="tpu_custom_call" | custom-call | bytes 1048576 | tf_op jit(solution)/shard_map/pallas_call | solution.py:104
  59.7 3.1 %collective-permute-start.6 = (bf16[512,512]{1,0:T(8,128)(2,1)}, bf16[512,512]{1,0:T(8,128)(2,1)S(1)}, u32[]{:S(2)}, u32[]{:S(2)}) collective-permute-start(bf16[512,512]{1,0:T(8,128)(2,1)} %shard_map.66.refs_4_.refs_5_), channel_id=1, source_target_pairs={{0,2},{1,3},{2,4},{3,5},{5,6},{8,9},{10,11},{12,13},{14,15},{13,14... | collective-permute-start | bytes 1572872 | tf_op jit(solution)/shard_map/ppermute | solution.py:418
  65.1 2.6 collective-permute-done.14.refs_2_
  67.7 3.4 %collective-permute-done.15.refs_3_ = bf16[128,512]{1,0:T(8,128)(2,1)S(1)} collective-permute-done((bf16[128,512]{1,0:T(8,128)(2,1)S(1)}, bf16[128,512]{1,0:T(8,128)(2,1)S(1)}, u32[]{:S(2)}, u32[]{:S(2)}) %collective-permute-start.15) | collective-permute-done | bytes 131104 | tf_op jit(solution)/shard_map/ppermute | solution.py:352
  71.7 17.0 %shard_map.69.refs_4_.refs_5_ = bf16[512,512]{1,0:T(8,128)(2,1)} custom-call(s32[1]{0:T(128)} %bitcast.head_ref, bf16[128,512]{1,0:T(8,128)(2,1)} %get-tuple-element.43.refs_0_, bf16[128,512]{1,0:T(8,128)(2,1)} %copy-done.15, bf16[128,512]{1,0:T(8,128)(2,1)} %copy-done.16, bf16[128,512]{1,0:T(8,128)(2,1)} %copy-done.17), custom_call_target="tpu_custom_call" | custom-call | bytes 1048576 | tf_op jit(solution)/shard_map/pallas_call | solution.py:104
  88.7 3.6 %collective-permute-start.16 = (bf16[512,512]{1,0:T(8,128)(2,1)}, bf16[512,512]{1,0:T(8,128)(2,1)S(1)}, u32[]{:S(2)}, u32[]{:S(2)}) collective-permute-start(bf16[512,512]{1,0:T(8,128)(2,1)} %shard_map.69.refs_4_.refs_5_), channel_id=1, source_target_pairs={{0,2},{1,3},{2,4},{3,5},{5,6},{8,9},{10,11},{12,13},{14,15},{9,12}... | collective-permute-start | bytes 1572872 | tf_op jit(solution)/shard_map/ppermute | solution.py:418
  96.6 9.5 %collective-permute-done.16.refs_6_.refs_7_ = bf16[512,512]{1,0:T(8,128)(2,1)S(1)} collective-permute-done((bf16[512,512]{1,0:T(8,128)(2,1)}, bf16[512,512]{1,0:T(8,128)(2,1)S(1)}, u32[]{:S(2)}, u32[]{:S(2)}) %collective-permute-start.16) | collective-permute-done | bytes 524320 | tf_op jit(solution)/shard_map/ppermute | solution.py:418
  108.2 6.1 %collective-permute-start.8 = (bf16[512,512]{1,0:T(8,128)(2,1)}, bf16[512,512]{1,0:T(8,128)(2,1)S(1)}, u32[]{:S(2)}, u32[]{:S(2)}) collective-permute-start(bf16[512,512]{1,0:T(8,128)(2,1)} %collective-permute-done.7.refs_8_.refs_9_), channel_id=1, source_target_pairs={{1,3},{2,4},{3,5},{10,11},{11,10},{12,13},{13,12},{17,19},{18,20},... | collective-permute-start | bytes 1572872 | tf_op jit(solution)/shard_map/ppermute | solution.py:418
  114.2 3.0 %collective-permute-done.17.refs_8_.refs_9_ = bf16[512,512]{1,0:T(8,128)(2,1)} collective-permute-done((bf16[512,512]{1,0:T(8,128)(2,1)S(1)}, bf16[512,512]{1,0:T(8,128)(2,1)}, u32[]{:S(2)}, u32[]{:S(2)}) %collective-permute-start.17) | collective-permute-done | bytes 524320 | tf_op jit(solution)/shard_map/ppermute | solution.py:418
  117.2 2.9 %collective-permute-start.18 = (bf16[512,512]{1,0:T(8,128)(2,1)}, bf16[512,512]{1,0:T(8,128)(2,1)S(1)}, u32[]{:S(2)}, u32[]{:S(2)}) collective-permute-start(bf16[512,512]{1,0:T(8,128)(2,1)} %collective-permute-done.17.refs_8_.refs_9_), channel_id=1, source_target_pairs={{1,3},{2,4},{3,5},{10,11},{11,10},{12,13},{13,12},{17,19},{18,20},... | collective-permute-start | bytes 1572872 | tf_op jit(solution)/shard_map/ppermute | solution.py:418
  120.1 32.9 %shard_map.64 = (bf16[128,1024]{1,0:T(8,128)(2,1)}, bf16[128,1024]{1,0:T(8,128)(2,1)}, bf16[128,1024]{1,0:T(8,128)(2,1)}, bf16[128,1024]{1,0:T(8,128)(2,1)}) custom-call(s32[1]{0:T(128)} %bitcast.head_ref, bf16[128,4096]{1,0:T(8,128)(2,1)} %refs_0_.2), custom_call_target="tpu_custom_call" | custom-call | bytes 2097152 | tf_op jit(solution)/shard_map/pallas_call | solution.py:104
  153.1 6.8 %collective-permute-start = (bf16[128,1024]{1,0:T(8,128)(2,1)}, bf16[128,1024]{1,0:T(8,128)(2,1)S(1)}, u32[]{:S(2)}, u32[]{:S(2)}) collective-permute-start(bf16[128,1024]{1,0:T(8,128)(2,1)} %get-tuple-element.30), channel_id=1, source_target_pairs={{0,8},{8,0},{16,24},{24,16},{1,9},{9,1},{17,25},{25,17},{2,10},{10... | collective-permute-start | bytes 786440 | tf_op jit(solution)/shard_map/ppermute | solution.py:352
  165.3 2.5 pad_add_fusion.2
  168.0 5.8 %collective-permute-done.2.refs_3_ = bf16[128,1024]{1,0:T(8,128)(2,1)S(1)} collective-permute-done((bf16[128,1024]{1,0:T(8,128)(2,1)}, bf16[128,1024]{1,0:T(8,128)(2,1)S(1)}, u32[]{:S(2)}, u32[]{:S(2)}) %collective-permute-start.2) | collective-permute-done | bytes 262176 | tf_op jit(solution)/shard_map/ppermute | solution.py:352
  175.7 19.8 %shard_map.70 = (f32[512,512]{1,0:T(8,128)S(1)}, f32[512,512]{1,0:T(8,128)S(1)}) custom-call(s32[4]{0:T(128)S(1)} %get-tuple-element.63.meta_ref, s32[4096]{0:T(1024)S(1)} %copy-done.6, s32[32]{0:T(128)S(1)} %reshape.27.read_ref, bf16[128,1024]{1,0:T(8,128)(2,1)S(1)} %copy-done.2, bf16[128,1024]{1,0:T(8,128)(2,1)S(1)} %collective-permute-done.refs_1_, ...), custom_call_target="tpu_custom_call" | custom-call | flops 1610612736 | bytes 1048576 | tf_op jit(solution)/shard_map/pallas_call | solution.py:287
  195.5 8.0 %shard_map.71 = (bf16[128,512]{1,0:T(8,128)(2,1)S(1)}, bf16[128,512]{1,0:T(8,128)(2,1)S(1)}, bf16[128,512]{1,0:T(8,128)(2,1)S(1)}, bf16[128,512]{1,0:T(8,128)(2,1)S(1)}) custom-call(s32[3]{0:T(128)S(1)} %pad_add_fusion.3.meta_ref, s32[4096]{0:T(1024)S(1)} %copy-done.6, s32[32]{0:T(128)S(1)} %reshape.27.read_ref, bf16[128,1024]{1,0:T(8,128)(2,1)S(1)} %copy-done.3, ...), custom_call_target="tpu_custom_call" | custom-call | flops 536870912 | bytes 1048576 | tf_op jit(solution)/shard_map/pallas_call | solution.py:287
  203.9 14.1 %shard_map.67 = (f32[512,512]{1,0:T(8,128)S(1)}, f32[512,512]{1,0:T(8,128)S(1)}) custom-call(s32[4]{0:T(128)S(1)} %get-tuple-element.62.meta_ref, s32[4096]{0:T(1024)S(1)} %copy-done.6, s32[32]{0:T(128)S(1)} %reshape.27.read_ref, bf16[128,1024]{1,0:T(8,128)(2,1)S(1)} %copy-done.3, bf16[128,1024]{1,0:T(8,128)(2,1)S(1)} %collective-permute-done.refs_1_, ...), custom_call_target="tpu_custom_call" | custom-call | flops 1610612736 | bytes 1048576 | tf_op jit(solution)/shard_map/pallas_call | solution.py:287
  218.3 7.5 %collective-permute-start.21 = (bf16[128,512]{1,0:T(8,128)(2,1)S(1)}, bf16[128,512]{1,0:T(8,128)(2,1)S(1)}, u32[]{:S(2)}, u32[]{:S(2)}) collective-permute-start(bf16[128,512]{1,0:T(8,128)(2,1)S(1)} %get-tuple-element.52), channel_id=1, source_target_pairs={{0,24},{8,16},{16,8},{24,0},{1,25},{9,17},{17,9},{25,1},{2,26},{10... | collective-permute-start | bytes 393224 | tf_op jit(solution)/shard_map/ppermute | solution.py:352
  225.8 14.1 %shard_map.68 = (bf16[128,512]{1,0:T(8,128)(2,1)S(1)}, bf16[128,512]{1,0:T(8,128)(2,1)S(1)}, bf16[128,512]{1,0:T(8,128)(2,1)S(1)}, bf16[128,512]{1,0:T(8,128)(2,1)S(1)}) custom-call(s32[4]{0:T(128)S(1)} %pad_add_fusion.meta_ref, s32[4096]{0:T(1024)S(1)} %copy-done.6, s32[32]{0:T(128)S(1)} %reshape.27.read_ref, bf16[128,1024]{1,0:T(8,128)(2,1)S(1)} %copy-done.3, ...), custom_call_target="tpu_custom_call" | custom-call | flops 1073741824 | bytes 1048576 | tf_op jit(solution)/shard_map/pallas_call | solution.py:287
  245.1 3.5 %collective-permute-done.12.refs_3_ = bf16[128,512]{1,0:T(8,128)(2,1)S(1)} collective-permute-done((bf16[128,512]{1,0:T(8,128)(2,1)S(1)}, bf16[128,512]{1,0:T(8,128)(2,1)S(1)}, u32[]{:S(2)}, u32[]{:S(2)}) %collective-permute-start.12) | collective-permute-done | bytes 131104 | tf_op jit(solution)/shard_map/ppermute | solution.py:352
  249.2 32.9 %shard_map.72 = bf16[128,4096]{1,0:T(8,128)(2,1)} custom-call(s32[1]{0:T(128)} %bitcast.head_ref, bf16[128,512]{1,0:T(8,128)(2,1)} %copy-done.8, bf16[128,512]{1,0:T(8,128)(2,1)} %copy-done.12, bf16[128,512]{1,0:T(8,128)(2,1)} %copy-done.13, bf16[128,512]{1,0:T(8,128)(2,1)} %copy-done.14, bf16[128,512]{1,0:T(8,128)(2,1)} %copy-done.7, ...), custom_call_target="tpu_custom_call" | custom-call | bytes 2097152 | tf_op jit(solution)/shard_map/pallas_call | solution.py:104
  (88 shorter events, 24.9 us)
Async XLA Ops:
  33.0 2.5 collective-permute-start.3
  33.8 5.3 %collective-permute-start.4 = (bf16[128,512]{1,0:T(8,128)(2,1)}, bf16[128,512]{1,0:T(8,128)(2,1)S(1)}, u32[]{:S(2)}, u32[]{:S(2)}) collective-permute-start(bf16[128,512]{1,0:T(8,128)(2,1)} %get-tuple-element.35), channel_id=1, source_target_pairs={{0,16},{8,24},{16,0},{24,8},{1,17},{9,25},{17,1},{25,9},{2,18},{10... | collective-permute-start | bytes 393224 | tf_op jit(solution)/shard_map/ppermute | solution.py:352
  34.0 8.0 %collective-permute-start.5 = (bf16[128,512]{1,0:T(8,128)(2,1)}, bf16[128,512]{1,0:T(8,128)(2,1)S(1)}, u32[]{:S(2)}, u32[]{:S(2)}) collective-permute-start(bf16[128,512]{1,0:T(8,128)(2,1)} %get-tuple-element.36), channel_id=1, source_target_pairs={{0,24},{8,16},{16,8},{24,0},{1,25},{9,17},{17,9},{25,1},{2,26},{10... | collective-permute-start | bytes 393224 | tf_op jit(solution)/shard_map/ppermute | solution.py:352
  42.7 20.6 %copy-start.22 = (bf16[128,512]{1,0:T(8,128)(2,1)S(1)}, bf16[128,512]{1,0:T(8,128)(2,1)}, u32[]{:S(2)}) copy-start(bf16[128,512]{1,0:T(8,128)(2,1)} %get-tuple-element.46) | copy-start | bytes 393220
  59.7 34.7 %collective-permute-start.6 = (bf16[512,512]{1,0:T(8,128)(2,1)}, bf16[512,512]{1,0:T(8,128)(2,1)S(1)}, u32[]{:S(2)}, u32[]{:S(2)}) collective-permute-start(bf16[512,512]{1,0:T(8,128)(2,1)} %shard_map.66.refs_4_.refs_5_), channel_id=1, source_target_pairs={{0,2},{1,3},{2,4},{3,5},{5,6},{8,9},{10,11},{12,13},{14,15},{13,14... | collective-permute-start | bytes 1572872 | tf_op jit(solution)/shard_map/ppermute | solution.py:418
  62.9 2.2 collective-permute-start.13
  62.9 4.7 %collective-permute-start.14 = (bf16[128,512]{1,0:T(8,128)(2,1)S(1)}, bf16[128,512]{1,0:T(8,128)(2,1)S(1)}, u32[]{:S(2)}, u32[]{:S(2)}) collective-permute-start(bf16[128,512]{1,0:T(8,128)(2,1)S(1)} %copy-done.23), channel_id=1, source_target_pairs={{0,16},{8,24},{16,0},{24,8},{1,17},{9,25},{17,1},{25,9},{2,18},{10... | collective-permute-start | bytes 393224 | tf_op jit(solution)/shard_map/ppermute | solution.py:352
  63.2 7.8 %collective-permute-start.15 = (bf16[128,512]{1,0:T(8,128)(2,1)S(1)}, bf16[128,512]{1,0:T(8,128)(2,1)S(1)}, u32[]{:S(2)}, u32[]{:S(2)}) collective-permute-start(bf16[128,512]{1,0:T(8,128)(2,1)S(1)} %copy-done.22), channel_id=1, source_target_pairs={{0,24},{8,16},{16,8},{24,0},{1,25},{9,17},{17,9},{25,1},{2,26},{10... | collective-permute-start | bytes 393224 | tf_op jit(solution)/shard_map/ppermute | solution.py:352
  71.7 22.7 %copy-start = (bf16[512,512]{1,0:T(8,128)(2,1)S(1)}, bf16[512,512]{1,0:T(8,128)(2,1)}, u32[]{:S(2)}) copy-start(bf16[512,512]{1,0:T(8,128)(2,1)} %shard_map.66.refs_4_.refs_5_) | copy-start | bytes 1572868
  88.7 17.4 %collective-permute-start.16 = (bf16[512,512]{1,0:T(8,128)(2,1)}, bf16[512,512]{1,0:T(8,128)(2,1)S(1)}, u32[]{:S(2)}, u32[]{:S(2)}) collective-permute-start(bf16[512,512]{1,0:T(8,128)(2,1)} %shard_map.69.refs_4_.refs_5_), channel_id=1, source_target_pairs={{0,2},{1,3},{2,4},{3,5},{5,6},{8,9},{10,11},{12,13},{14,15},{9,12}... | collective-permute-start | bytes 1572872 | tf_op jit(solution)/shard_map/ppermute | solution.py:418
  94.5 13.7 %collective-permute-start.7 = (bf16[512,512]{1,0:T(8,128)(2,1)S(1)}, bf16[512,512]{1,0:T(8,128)(2,1)}, u32[]{:S(2)}, u32[]{:S(2)}) collective-permute-start(bf16[512,512]{1,0:T(8,128)(2,1)S(1)} %broadcast_select_fusion.1), channel_id=1, source_target_pairs={{0,1},{2,3},{3,2},{4,5},{5,4},{6,7},{8,10},{9,11},{10,12},{11,13},... | collective-permute-start | bytes 1572872 | tf_op jit(solution)/shard_map/ppermute | solution.py:418
  106.9 10.3 %collective-permute-start.17 = (bf16[512,512]{1,0:T(8,128)(2,1)S(1)}, bf16[512,512]{1,0:T(8,128)(2,1)}, u32[]{:S(2)}, u32[]{:S(2)}) collective-permute-start(bf16[512,512]{1,0:T(8,128)(2,1)S(1)} %broadcast_select_fusion), channel_id=1, source_target_pairs={{0,1},{2,3},{3,2},{4,5},{5,4},{6,7},{8,10},{9,11},{10,12},{11,13},... | collective-permute-start | bytes 1572872 | tf_op jit(solution)/shard_map/ppermute | solution.py:418
  108.2 54.3 %collective-permute-start.8 = (bf16[512,512]{1,0:T(8,128)(2,1)}, bf16[512,512]{1,0:T(8,128)(2,1)S(1)}, u32[]{:S(2)}, u32[]{:S(2)}) collective-permute-start(bf16[512,512]{1,0:T(8,128)(2,1)} %collective-permute-done.7.refs_8_.refs_9_), channel_id=1, source_target_pairs={{1,3},{2,4},{3,5},{10,11},{11,10},{12,13},{13,12},{17,19},{18,20},... | collective-permute-start | bytes 1572872 | tf_op jit(solution)/shard_map/ppermute | solution.py:418
  117.2 78.3 %collective-permute-start.18 = (bf16[512,512]{1,0:T(8,128)(2,1)}, bf16[512,512]{1,0:T(8,128)(2,1)S(1)}, u32[]{:S(2)}, u32[]{:S(2)}) collective-permute-start(bf16[512,512]{1,0:T(8,128)(2,1)} %collective-permute-done.17.refs_8_.refs_9_), channel_id=1, source_target_pairs={{1,3},{2,4},{3,5},{10,11},{11,10},{12,13},{13,12},{17,19},{18,20},... | collective-permute-start | bytes 1572872 | tf_op jit(solution)/shard_map/ppermute | solution.py:418
  153.1 14.7 %collective-permute-start = (bf16[128,1024]{1,0:T(8,128)(2,1)}, bf16[128,1024]{1,0:T(8,128)(2,1)S(1)}, u32[]{:S(2)}, u32[]{:S(2)}) collective-permute-start(bf16[128,1024]{1,0:T(8,128)(2,1)} %get-tuple-element.30), channel_id=1, source_target_pairs={{0,8},{8,0},{16,24},{24,16},{1,9},{9,1},{17,25},{25,17},{2,10},{10... | collective-permute-start | bytes 786440 | tf_op jit(solution)/shard_map/ppermute | solution.py:352
  159.9 8.1 %collective-permute-start.1 = (bf16[128,1024]{1,0:T(8,128)(2,1)}, bf16[128,1024]{1,0:T(8,128)(2,1)S(1)}, u32[]{:S(2)}, u32[]{:S(2)}) collective-permute-start(bf16[128,1024]{1,0:T(8,128)(2,1)} %get-tuple-element.31), channel_id=1, source_target_pairs={{0,16},{8,24},{16,0},{24,8},{1,17},{9,25},{17,1},{25,9},{2,18},{10... | collective-permute-start | bytes 786440 | tf_op jit(solution)/shard_map/ppermute | solution.py:352
  160.1 13.6 %collective-permute-start.2 = (bf16[128,1024]{1,0:T(8,128)(2,1)}, bf16[128,1024]{1,0:T(8,128)(2,1)S(1)}, u32[]{:S(2)}, u32[]{:S(2)}) collective-permute-start(bf16[128,1024]{1,0:T(8,128)(2,1)} %get-tuple-element.32), channel_id=1, source_target_pairs={{0,24},{8,16},{16,8},{24,0},{1,25},{9,17},{17,9},{25,1},{2,26},{10... | collective-permute-start | bytes 786440 | tf_op jit(solution)/shard_map/ppermute | solution.py:352
  162.5 63.3 %collective-permute-start.9 = (bf16[512,512]{1,0:T(8,128)(2,1)S(1)}, bf16[512,512]{1,0:T(8,128)(2,1)S(1)}, u32[]{:S(2)}, u32[]{:S(2)}) collective-permute-start(bf16[512,512]{1,0:T(8,128)(2,1)S(1)} %collective-permute-done.8.refs_4_.refs_5_), channel_id=1, source_target_pairs={{10,12},{26,28}} | collective-permute-start | bytes 1572872 | tf_op jit(solution)/shard_map/ppermute | solution.py:418
  203.6 37.2 %collective-permute-start.19 = (bf16[128,512]{1,0:T(8,128)(2,1)S(1)}, bf16[128,512]{1,0:T(8,128)(2,1)S(1)}, u32[]{:S(2)}, u32[]{:S(2)}) collective-permute-start(bf16[128,512]{1,0:T(8,128)(2,1)S(1)} %get-tuple-element.50), channel_id=1, source_target_pairs={{0,8},{8,0},{16,24},{24,16},{1,9},{9,1},{17,25},{25,17},{2,10},{10... | collective-permute-start | bytes 393224 | tf_op jit(solution)/shard_map/ppermute | solution.py:352
  218.0 24.7 %collective-permute-start.20 = (bf16[128,512]{1,0:T(8,128)(2,1)S(1)}, bf16[128,512]{1,0:T(8,128)(2,1)S(1)}, u32[]{:S(2)}, u32[]{:S(2)}) collective-permute-start(bf16[128,512]{1,0:T(8,128)(2,1)S(1)} %get-tuple-element.51), channel_id=1, source_target_pairs={{0,16},{8,24},{16,0},{24,8},{1,17},{9,25},{17,1},{25,9},{2,18},{10... | collective-permute-start | bytes 393224 | tf_op jit(solution)/shard_map/ppermute | solution.py:352
  218.3 24.4 %collective-permute-start.21 = (bf16[128,512]{1,0:T(8,128)(2,1)S(1)}, bf16[128,512]{1,0:T(8,128)(2,1)S(1)}, u32[]{:S(2)}, u32[]{:S(2)}) collective-permute-start(bf16[128,512]{1,0:T(8,128)(2,1)S(1)} %get-tuple-element.52), channel_id=1, source_target_pairs={{0,24},{8,16},{16,8},{24,0},{1,25},{9,17},{17,9},{25,1},{2,26},{10... | collective-permute-start | bytes 393224 | tf_op jit(solution)/shard_map/ppermute | solution.py:352
  240.5 2.2 collective-permute-start.10
  240.6 4.6 %collective-permute-start.11 = (bf16[128,512]{1,0:T(8,128)(2,1)S(1)}, bf16[128,512]{1,0:T(8,128)(2,1)S(1)}, u32[]{:S(2)}, u32[]{:S(2)}) collective-permute-start(bf16[128,512]{1,0:T(8,128)(2,1)S(1)} %get-tuple-element.41), channel_id=1, source_target_pairs={{0,16},{8,24},{16,0},{24,8},{1,17},{9,25},{17,1},{25,9},{2,18},{10... | collective-permute-start | bytes 393224 | tf_op jit(solution)/shard_map/ppermute | solution.py:352
  240.8 7.8 %collective-permute-start.12 = (bf16[128,512]{1,0:T(8,128)(2,1)S(1)}, bf16[128,512]{1,0:T(8,128)(2,1)S(1)}, u32[]{:S(2)}, u32[]{:S(2)}) collective-permute-start(bf16[128,512]{1,0:T(8,128)(2,1)S(1)} %get-tuple-element.42), channel_id=1, source_target_pairs={{0,24},{8,16},{16,8},{24,0},{1,25},{9,17},{17,9},{25,1},{2,26},{10... | collective-permute-start | bytes 393224 | tf_op jit(solution)/shard_map/ppermute | solution.py:352
  (23 other events, 150.3 us)

commit v2 on v0

v2 whole, which is shorter than its diff:
```python
import functools
import math

import jax
import jax.numpy as jnp
from jax import lax
from jax.experimental import pallas as pl
from jax.experimental.pallas import tpu as pltpu
from jax.sharding import PartitionSpec as P

QUERY_HEADS = 32
KEY_VALUE_HEADS = 16
HEAD_WIDTH = 128
GROUP = QUERY_HEADS // KEY_VALUE_HEADS

log_scale = 168.0 ** (-0.5) * math.log2(math.e)
neg_large = -1e30
SMALL_VMEM = 4 * 1024 * 1024


def wanted_blocks(count, window):
    middle = count // 2
    whole = set(range(window)) | set(range(max(middle - window, 0), middle + 1))
    return [
        [b for b in range(max(0, t - window + 1), t) if all(m in whole for m in range(b + 1, t))]
        for t in range(count)
    ]


def plan_rounds(count, window, kind, direct):
    wanted = wanted_blocks(count, window)
    held = [{c: 0} for c in range(count)]
    rounds = []

    def missing(t):
        return [b for b in wanted[t] if b not in held[t]]

    def send(k, s, t, b):
        rounds[k][t] = (s, b, held[s][b])
        held[t][b] = k + 1

    def free(k, s, t):
        return t not in rounds[k] and all(entry[0] != s for entry in rounds[k].values())

    for k in range(3):
        rounds.append({})
        had = [dict(x) for x in held]
        for s in range(count):
            t = s + 2 if (k + kind) % 2 == 0 else s ^ 1
            if t >= count:
                continue
            choice = [b for b in had[s] if b in missing(t)]
            if choice:
                send(k, s, t, max(choice))
    for t in range(count):
        for b in missing(t):
            options = [
                (k, b) for k in range(3) if t - b == 1 and (k + kind) % 2 == 0 and free(k, b, t)
            ]
            k = 3
            while not options:
                if k == len(rounds):
                    rounds.append({})
                holders = [s for s in range(count) if held[s].get(b, k + 1) <= k and free(k, s, t)]
                if direct:
                    holders = [s for s in holders if s == b]
                holders.sort(key=lambda s: (abs(t - s) != 2, abs(t - s)))
                options = [(k, s) for s in holders]
                k += 1
            send(options[0][0], options[0][1], t, b)
    return rounds


in_smem = pl.BlockSpec(memory_space=pltpu.SMEM)
in_vmem = pl.BlockSpec(memory_space=pltpu.VMEM)
anywhere = pl.BlockSpec(memory_space=pl.ANY)
in_hbm = pl.BlockSpec(memory_space=pltpu.HBM)


def move(place, operands, copies, shapes, source_spec, target_spec, after=(), weight=1):
    count_in = len(operands)

    def kernel(place_ref, *refs):
        h = place_ref[1]
        sources, targets, sems = refs[:count_in], refs[count_in + len(after) : -1], refs[-1]

        def span(value, size):
            return pl.ds(pl.multiple_of(value(h), 128) if callable(value) else value, size)

        started = []
        for number, (s, row, rows, col, cols, t, to_row, to_col) in enumerate(copies):
            copy = pltpu.make_async_copy(
                sources[s].at[span(row, rows), span(col, cols)],
                targets[t].at[span(to_row, rows), span(to_col, cols)],
                sems.at[number],
            )
            copy.start()
            started.append(copy)
        for copy in started:
            copy.wait()

    return pl.pallas_call(
        kernel,
        out_shape=[jax.ShapeDtypeStruct(s, jnp.bfloat16) for s in shapes],
        in_specs=[in_smem] + [source_spec] * count_in + [anywhere] * len(after),
        out_specs=[target_spec] * len(shapes),
        scratch_shapes=[pltpu.SemaphoreType.DMA((len(copies),))],
        compiler_params=pltpu.CompilerParams(
            vmem_limit_bytes=SMALL_VMEM
        ),
        cost_estimate=pl.CostEstimate(
            flops=0,
            bytes_accessed=weight * sum(4 * c[2] * c[4] for c in copies),
            transcendentals=0,
        ),
    )(place, *operands, *after)


def survey(place, table, documents, readers, entries, rounds, window, slots, rows):
    def kernel(place_ref, table_ref, doc_ref, read_ref, out_ref):
        ctx, head = place_ref[0], place_ref[1]
        out_ref[0] = ctx
        out_ref[1] = head
        base = (ctx * slots + head) * entries
        q_first, q_last = doc_ref[ctx * rows], doc_ref[ctx * rows + rows - 1]
        for k in range(rounds):
            number = table_ref[base + k]
            block = jnp.maximum(number, 0)
            k_first, k_last = doc_ref[block * rows], doc_ref[block * rows + rows - 1]
            distance = jnp.clip(ctx - block, 0, window - 1)
            live = (
                (number >= 0) & (read_ref[block * window + distance] > 0) & (k_last == q_first)
            )
            out_ref[2 + 3 * k] = block
            out_ref[3 + 3 * k] = live.astype(jnp.int32)
            out_ref[4 + 3 * k] = (k_first == q_last).astype(jnp.int32)
        for k in range(rounds, entries):
            out_ref[2 + 2 * rounds + k] = table_ref[base + k]

    return pl.pallas_call(
        kernel,
        out_shape=jax.ShapeDtypeStruct((2 + 2 * rounds + entries,), jnp.int32),
        in_specs=[in_smem] * 4,
        out_specs=in_smem,
        compiler_params=pltpu.CompilerParams(vmem_limit_bytes=SMALL_VMEM),
    )(place, table, documents, readers)


def choose(info, entry, candidates, after=()):
    numbers = sorted(candidates)

    def kernel(info_ref, *refs):
        named = info_ref[entry]

        @pl.when(named <= numbers[0])
        def _():
            refs[-1][...] = refs[0][...]

        for number, ref in zip(numbers[1:], refs[1 : len(numbers)]):

            @pl.when(named == number)
            def _(ref=ref):
                refs[-1][...] = ref[...]

    first = candidates[numbers[0]]
    return pl.pallas_call(
        kernel,
        out_shape=jax.ShapeDtypeStruct(first.shape, first.dtype),
        in_specs=[in_smem] + [in_vmem] * len(numbers) + [anywhere] * len(after),
        out_specs=in_vmem,
        compiler_params=pltpu.CompilerParams(vmem_limit_bytes=SMALL_VMEM),
        cost_estimate=pl.CostEstimate(
            flops=0, bytes_accessed=4 * first.size, transcendentals=0
        ),
    )(info, *[candidates[n] for n in numbers], *after)


def attend(info, doc_rows, queries, heads, blocks, chosen, state, final):
    slots = len(queries)
    arrays = list({id(array): array for array, _ in queries}.values())
    spots = [([id(a) for a in arrays].index(id(array)), row) for array, row in queries]
    sizes = [part.shape[0] for part in blocks[0]]
    rows = sum(sizes)
    tokens = rows // slots
    all_heads = arrays[0].shape[1] // (GROUP * HEAD_WIDTH)
    count = len(blocks)
    stacked = all_heads * GROUP * rows
    parts = len(sizes)
    with_own = state is None

    def kernel(info_ref, rows_ref, *refs):
        q_refs, refs = refs[: len(arrays)], refs[len(arrays) :]
        kv_refs, refs = refs[: count * parts], refs[count * parts :]
        if final:
            acc, top, *out_refs = refs[:-4]
        else:
            acc, top = refs[-6:-4]
        held, bias, key_bias, query_mask = refs[-4:]
        ctx, head = info_ref[0], info_ref[1]
        chip = head - head % 2

        def docs_of(block, place):
            return rows_ref[pl.ds(block * slots + place, 1), :]

        def make_bias():
            def of_queries(i, _):
                place_q = head ^ i
                q_docs = jnp.broadcast_to(docs_of(ctx, place_q), (tokens, tokens)).T
                q_pos = place_q * tokens + lax.broadcasted_iota(jnp.int32, (tokens, tokens), 0)
                for j in range(slots):
                    place_k = chip ^ j
                    k_pos = place_k * tokens + lax.broadcasted_iota(jnp.int32, (tokens, tokens), 1)
                    seen = (q_docs == docs_of(ctx, place_k)) & (k_pos <= q_pos)
                    bias[
                        pl.ds(pl.multiple_of(i * tokens, tokens), tokens),
                        j * tokens : (j + 1) * tokens,
                    ] = jnp.where(seen, 0.0, neg_large)
                return 0

            lax.fori_loop(0, slots, of_queries, 0)

        def make_masks(block):
            first_doc = docs_of(ctx, 0)[:, 0:1]
            for j in range(slots):
                seen = docs_of(block, chip ^ j) == first_doc
                key_bias[:, j * tokens : (j + 1) * tokens] = jnp.where(seen, 0.0, neg_large)
                asks = (docs_of(ctx, head ^ j) == first_doc).astype(jnp.float32)
                query_mask[j * tokens : (j + 1) * tokens, :] = jnp.broadcast_to(
                    asks, (tokens, tokens)
                ).T

        def lanes_of(head):
            return pl.ds(pl.multiple_of(head * HEAD_WIDTH, HEAD_WIDTH), HEAD_WIDTH)

        def rows_of(n, r):
            return pl.ds(pl.multiple_of(n * rows + r * tokens, tokens), tokens)

        def load(index, kv_head):
            row = 0
            for ref, size in zip(kv_refs[index * parts : (index + 1) * parts], sizes):
                for column, source in enumerate((kv_head, all_heads + kv_head)):
                    held[row : row + size, column * HEAD_WIDTH : (column + 1) * HEAD_WIDTH] = ref[
                        :, lanes_of(source)
                    ]
                row += size

        def give(n, r, sums):
            out_refs[r][:, lanes_of(n - heads[0] * GROUP)] = (
                sums[:, :HEAD_WIDTH] / sums[:, HEAD_WIDTH:]
            ).astype(jnp.bfloat16)

        def tile(n, r, key, keys, masked, first):
            part = rows_of(n, r)
            array, row = spots[r]
            scores = lax.dot_general(
                q_refs[array][row : row + tokens, lanes_of(n)],
                held[key : key + keys, :HEAD_WIDTH],
                (((1,), (1,)), ((), ())),
                preferred_element_type=jnp.float32,
            )
            here = slice(r * tokens, (r + 1) * tokens)
            if first:
                scores = scores + bias[here, key : key + keys]
            elif masked:
                scores = scores + key_bias[...]
            peak = jnp.max(scores, axis=1, keepdims=True)
            peak = jnp.broadcast_to(peak, (tokens, HEAD_WIDTH))
            if not first:
                before = top[part, :]
                peak = jnp.maximum(peak, before)
            weights = jnp.exp2(
                (scores - jnp.concatenate([peak] * (keys // HEAD_WIDTH), axis=1)) * log_scale
            )
            sums = jnp.dot(
                weights.astype(jnp.bfloat16),
                held[key : key + keys, HEAD_WIDTH:],
                preferred_element_type=jnp.float32,
            )
            if not first:
                fade = jnp.exp2((before - peak) * log_scale)
                old = acc[part, :]
                sums = old * jnp.concatenate([fade, fade], axis=1) + sums
                if masked:
                    asks = query_mask[here, :] > 0.5
                    sums = jnp.where(jnp.concatenate([asks, asks], axis=1), sums, old)
                    peak = jnp.where(asks, peak, before)
            if final:
                give(n, r, sums)
            else:
                acc[part, :] = sums
                top[part, :] = peak

        def each_head(work):
            def body(kv_head, _):
                work(kv_head)
                return 0

            lax.fori_loop(heads[0], heads[-1] + 1, body, 0)

        def run(index, masked, first=False):
            def work(kv_head):
                load(index, kv_head)
                for g in range(GROUP):
                    for r in range(slots):
                        tile(kv_head * GROUP + g, r, 0, rows, masked, first)

            each_head(work)

        def run_own():
            make_bias()
            if slots != 4:
                run(0, True, True)
                return
            half = 2 * tokens

            def all_of(chip_first):
                def work(kv_head):
                    load(0, kv_head)
                    for g in range(GROUP):
                        for r in range(slots):
                            n = kv_head * GROUP + g
                            if chip_first == (r < 2):
                                tile(n, r, half * (r >= 2), half, True, True)
                            else:
                                tile(n, r, 0, rows, True, True)

                each_head(work)

            pl.when(chip == 0)(functools.partial(all_of, True))
            pl.when(chip != 0)(functools.partial(all_of, False))

        held[:, 2 * HEAD_WIDTH :] = jnp.ones((rows, HEAD_WIDTH), jnp.bfloat16)
        for index, slot in enumerate(chosen):
            if slot == 0:
                run_own()
                continue
            block, live, full = [info_ref[3 * slot - 1 + i] for i in range(3)]

            @pl.when((live != 0) & (full != 0))
            def _(index=index):
                run(index, False)

            @pl.when((live != 0) & (full == 0))
            def _(index=index, block=block):
                make_masks(block)
                run(index, True)

            if final:

                @pl.when(live == 0)
                def _():
                    def work(kv_head):
                        for n in (kv_head * GROUP + g for g in range(GROUP)):
                            for r in range(slots):
                                give(n, r, acc[rows_of(n, r), :])

                    each_head(work)

    operands = [info, doc_rows] + arrays + [part for block in blocks for part in block]
    aliases = {}
    if not with_own:
        if not final:
            aliases = {len(operands): 0, len(operands) + 1: 1}
        operands += list(state)
    if final:
        out_shape = [
            jax.ShapeDtypeStruct((tokens, len(heads) * GROUP * HEAD_WIDTH), jnp.bfloat16)
        ] * slots
    else:
        out_shape = [
            jax.ShapeDtypeStruct((stacked, 2 * HEAD_WIDTH), jnp.float32),
            jax.ShapeDtypeStruct((stacked, HEAD_WIDTH), jnp.float32),
        ]
    scores_made = len(heads) * GROUP * rows * rows * count
    scratch = 2 * 3 * rows * HEAD_WIDTH + 4 * rows * (2 * HEAD_WIDTH + rows * with_own)
    return pl.pallas_call(
        kernel,
        out_shape=out_shape,
        in_specs=[in_smem] + [in_vmem] * (len(operands) - 1),
        out_specs=[in_vmem] * len(out_shape),
        input_output_aliases=aliases,
        scratch_shapes=[
            pltpu.VMEM((rows, 3 * HEAD_WIDTH), jnp.bfloat16),
            pltpu.VMEM((rows, rows if with_own else HEAD_WIDTH), jnp.float32),
            pltpu.VMEM((1, rows), jnp.float32),
            pltpu.VMEM((rows, tokens), jnp.float32),
        ],
        compiler_params=pltpu.CompilerParams(vmem_limit_bytes=SMALL_VMEM + scratch),
        cost_estimate=pl.CostEstimate(
            flops=4 * scores_made * HEAD_WIDTH,
            bytes_accessed=4 * stacked * HEAD_WIDTH,
            transcendentals=scores_made,
        ),
    )(*operands)


def per_device(query_matrix, key_matrix, value_matrix, documents, readers):
    shards = lax.axis_size("ctx")
    slots = lax.axis_size("head")
    window = readers.shape[1]
    tokens = query_matrix.shape[0]
    local_keys = key_matrix.shape[1] // slots
    local_queries = GROUP * local_keys
    key_heads = local_keys // HEAD_WIDTH
    place = jnp.stack([lax.axis_index("ctx"), lax.axis_index("head")]).astype(jnp.int32)
    doc_rows = documents.reshape(shards * slots, tokens)
    groups = [g for g in (range(2), range(2, slots)) if len(g)]

    plans = [
        [plan_rounds(shards, window, kind, part == len(groups) - 1) for kind in (0, 1)]
        for part in range(len(groups))
    ]
    length = max(len(kind) for plan in plans for kind in plan)
    plans = [[kind + [{}] * (length - len(kind)) for kind in plan] for plan in plans]
    entries = length * (1 + len(plans))
    table = []
    for c in range(shards):
        for h in range(slots):
            brought = [
                [plan[h % 2][k][c][1] if c in plan[h % 2][k] else -1 for k in range(length)]
                for plan in plans
            ]
            assert all(blocks == brought[0] for blocks in brought)
            table += brought[0]
            for plan in plans:
                for k in range(length):
                    sends = [e[2] for e in plan[h % 2][k].values() if e[0] == c]
                    table.append(sends[0] if sends else -1)
    info = survey(
        place, jnp.array(table, jnp.int32), documents, readers.reshape(-1), entries, length, window,
        slots, slots * tokens,
    )

    def swap(value, r):
        return lax.ppermute(value, "head", [(h, h ^ r) for h in range(slots)])

    def exchanged(sources, widths, before=()):
        copies = []
        for r in range(slots):
            column = 0
            for source, width in enumerate(widths):
                target, row = (r, 0) if r < 2 else (1 + r // 2, r % 2 * tokens)
                copies.append(
                    (
                        source,
                        0,
                        tokens,
                        lambda h, r=r, width=width: (h ^ r) * width,
                        width,
                        target,
                        row,
                        column,
                    )
                )
                column += width
        shapes = [(tokens, sum(widths))] * 2 + [(2 * tokens, sum(widths))] * (slots // 2 - 1)
        pieces = move(place, sources, copies, shapes[: slots // 2 + 1], in_vmem, in_vmem)
        spots = {0: (pieces[0], 0), 1: (swap(pieces[1], 1), 0)}
        sent = pieces[2:]
        if before and sent:
            sent = lax.optimization_barrier((tuple(sent), *before))[0]
        for r in range(2, slots, 2):
            spots[r] = (swap(sent[r // 2 - 1], r), 0)
        return spots

    def shared(spots, after=()):
        for r in range(2, slots, 2):
            got = spots[r][0]
            if after:
                got = lax.optimization_barrier((got, *after))[0]
            spots[r] = (got, 0)
            spots[r + 1] = (swap(got[tokens:], 1), 0)

    def part_of(spots, group, after=()):
        return move(
            place,
            [spots[r][0] for r in group],
            [
                (
                    number,
                    spots[r][1],
                    tokens,
                    0,
                    2 * local_keys,
                    0,
                    lambda h, r=r: ((h % 2) ^ r) * tokens - group[0] * tokens,
                    0,
                )
                for number, r in enumerate(group)
            ],
            [(len(group) * tokens, 2 * local_keys)],
            in_vmem,
            in_vmem,
            after,
        )[0]

    def send(part, k, after=()):
        pairs, used = [], set()
        for h in range(slots):
            for target, (source, _, slot) in plans[part][h % 2][k].items():
                pairs.append((h * shards + source, h * shards + target))
                used.add(slot)
        if len(used) > 1:
            candidates = {slot: held[part][slot] for slot in used}
            operand = choose(info, 2 + 3 * length + part * length + k, candidates, after)
        else:
            operand = held[part][min(used)]
            if after:
                operand = lax.optimization_barrier((operand, *after))[0]
        held[part][k + 1] = lax.ppermute(operand, ("head", "ctx"), pairs)
        return operand

    def attended(heads, chosen, state, final=False):
        asked = [queries[r] for r in range(slots)]
        blocks = [[part[slot] for part in held] for slot in chosen]
        return attend(info, doc_rows, asked, heads, blocks, chosen, state, final)

    halves = [range(key_heads)]
    if key_heads % 2 == 0:
        halves = [range(key_heads // 2), range(key_heads // 2, key_heads)]
    later = range(1, len(groups))
    spots = exchanged([key_matrix, value_matrix], [local_keys] * 2)
    held = [{0: part_of(spots, groups[0])}]
    send(0, 0)
    send(0, 1)
    across = range(2, slots, 2)
    queries = exchanged([query_matrix], [local_queries], [spots[r][0] for r in across])
    arrived = [queries[r][0] for r in across]
    shared(spots, [queries[0][0], info])
    for part in later:
        held.append({0: part_of(spots, groups[part], [held[0][1]])})
        send(part, 0)
    shared(queries)
    send(0, 2, arrived)
    for part in later:
        send(part, 1, [held[0][2]])
        for k in range(3, length):
            send(part, k)
    state = attended(range(key_heads), [0, 1], None)
    for k in range(3, length):
        send(0, k, [state[1]])
    for part in later:
        extra = [held[part][k + 1] for k in range(3, length)]
        send(part, 2, [held[0][3]] + extra + [state[1]])
    state = attended(range(key_heads), [2] + list(range(4, length + 1)), state)
    results = []
    for heads in halves:
        outs = attended(heads, [3], state, True)
        results += [swap(outs[r], r) if r else outs[r] for r in range(slots)]
    half_queries = local_queries // len(halves)
    return move(
        place,
        results,
        [
            (
                number * slots + r,
                0,
                tokens,
                0,
                half_queries,
                0,
                0,
                lambda h, r=r, number=number: (h ^ r) * local_queries + number * half_queries,
            )
            for number in range(len(halves))
            for r in range(slots)
        ],
        [query_matrix.shape],
        in_vmem,
        anywhere,
    )[0]


def solution(mesh):
    placed = (
        P(("ctx", "head"), None),
        P(("ctx", "head"), None),
        P(("ctx", "head"), None),
        P(),
        P(),
    )
    return jax.shard_map(
        per_device, mesh=mesh, in_specs=placed, out_specs=P(("ctx", "head"), None), check_vma=False
    )
```

time: 159 us -> 86.8 us (0.55)
  the two profiles are of different devices: /device:TPU:24 before, /device:TPU:21 now
where the time goes in v2:
time: 86.8 us; the launch traced here: 85.3 us
  starting transfers between devices  31.4 us (36%)
  Pallas kernels  28.2 us (32%)
  waiting for transfers between devices  19.7 us (23%)
  local copies, waits for them, and re-layouts  5.58 us (6%)
    ppermute x8, starting transfers between devices, send(): held[part][k + 1] = lax.ppermute(operand, ('head', 'ctx'), pairs)  24.2 us
    pallas_call x4, Pallas kernels, attend(): pl.pallas_call(kernel, out_shape=out_shape, in_specs=[in_smem] + [in_vmem...  21.3 us
    ppermute x12, waiting for transfers between devices, swap(): return lax.ppermute(value, 'head', [(h, h ^ r) for h in range(slots)])  16.2 us
    ppermute x12, starting transfers between devices, swap(): return lax.ppermute(value, 'head', [(h, h ^ r) for h in range(slots)])  7.16 us
    unnamed x13, local copies, waits for them, and re-layouts  5.47 us
    pallas_call x5, Pallas kernels, move(): pl.pallas_call(kernel, out_shape=[jax.ShapeDtypeStruct(s, jnp.bfloat16) f...  4.25 us
    ppermute x8, waiting for transfers between devices, send(): held[part][k + 1] = lax.ppermute(operand, ('head', 'ctx'), pairs)  3.47 us
  transfers between devices with their start and end apart: 20, of which 7 were waited for; matrix products, arithmetic and copies ran while one was open for 1% of the time, Pallas kernels for 27%

profile of v2, /device:TPU:21, one launch (start us, length us, event | category | flops | bytes accessed | tf_op | source)
XLA Modules:
  0.0 85.3 jit_solution(6225061840833116209)
XLA Ops:
  0.1 1.0 %copy-done.1 = bf16[128,2048]{1,0:T(8,128)(2,1)S(1)} copy-done((bf16[128,2048]{1,0:T(8,128)(2,1)S(1)}, bf16[128,2048]{1,0:T(8,128)(2,1)}, u32[]{:S(2)}) %copy-start.1) | copy-done | bytes 524312
  5.5 3.1 %collective-permute-start.5 = (bf16[256,1024]{1,0:T(8,128)(2,1)S(1)}, bf16[256,1024]{1,0:T(8,128)(2,1)S(1)}, u32[]{:S(2)}, u32[]{:S(2)}) collective-permute-start(bf16[256,1024]{1,0:T(8,128)(2,1)S(1)} %shard_map.67.refs_0_.refs_4_), channel_id=1, source_target_pairs={{0,2},{1,3},{2,4},{3,5},{5,6},{8,9},{10,11},{12,13},{14,15},{16,18... | collective-permute-start | bytes 1572872 | tf_op jit(solution)/shard_map/ppermute | solution.py:510
  8.6 1.2 %copy-done = bf16[128,4096]{1,0:T(8,128)(2,1)S(1)} copy-done((bf16[128,4096]{1,0:T(8,128)(2,1)S(1)}, bf16[128,4096]{1,0:T(8,128)(2,1)}, u32[]{:S(2)}) %copy-start) | copy-done | bytes 1048600
  12.8 1.5 %shard_map.64.info_ref = s32[22]{0:T(128)S(1)} custom-call(s32[2]{0:T(128)S(1)} %pad_add_fusion.place_ref, s32[384]{0:T(512)S(1)} %copy-done.5, s32[4096]{0:T(1024)S(1)} %copy-done.3, s32[32]{0:T(128)S(1)} %reshape.6.read_ref), custom_call_target="tpu_custom_call" | custom-call | tf_op jit(solution)/shard_map/pallas_call | solution.py:140
  14.3 2.9 %collective-permute-done.1.refs_0_ = bf16[256,1024]{1,0:T(8,128)(2,1)S(1)} collective-permute-done((bf16[256,1024]{1,0:T(8,128)(2,1)S(1)}, bf16[256,1024]{1,0:T(8,128)(2,1)S(1)}, u32[]{:S(2)}, u32[]{:S(2)}) %collective-permute-start.1) | collective-permute-done | bytes 524320 | tf_op jit(solution)/shard_map/ppermute | solution.py:435
  19.0 1.3 %collective-permute-start.6 = (bf16[256,1024]{1,0:T(8,128)(2,1)S(1)}, bf16[256,1024]{1,0:T(8,128)(2,1)S(1)}, u32[]{:S(2)}, u32[]{:S(2)}) collective-permute-start(bf16[256,1024]{1,0:T(8,128)(2,1)S(1)} %shard_map.68), channel_id=1, source_target_pairs={{0,1},{2,3},{3,2},{4,5},{5,4},{6,7},{8,10},{9,11},{10,12},{11,13},... | collective-permute-start | bytes 1572872 | tf_op jit(solution)/shard_map/ppermute | solution.py:510
  20.9 5.0 %collective-permute-start.9 = (bf16[256,1024]{1,0:T(8,128)(2,1)S(1)}, bf16[256,1024]{1,0:T(8,128)(2,1)S(1)}, u32[]{:S(2)}, u32[]{:S(2)}) collective-permute-start(bf16[256,1024]{1,0:T(8,128)(2,1)S(1)} %shard_map.69.refs_0_.refs_5_), channel_id=1, source_target_pairs={{0,2},{1,3},{2,4},{3,5},{5,6},{8,9},{10,11},{12,13},{14,15},{16,18... | collective-permute-start | bytes 1572872 | tf_op jit(solution)/shard_map/ppermute | solution.py:510
  25.9 5.7 %collective-permute-done.2.refs_2_ = bf16[256,1024]{1,0:T(8,128)(2,1)S(1)} collective-permute-done((bf16[256,1024]{1,0:T(8,128)(2,1)S(1)}, bf16[256,1024]{1,0:T(8,128)(2,1)S(1)}, u32[]{:S(2)}, u32[]{:S(2)}) %collective-permute-start.2) | collective-permute-done | bytes 524320 | tf_op jit(solution)/shard_map/ppermute | solution.py:435
  31.6 3.1 %collective-permute-start.7 = (bf16[256,1024]{1,0:T(8,128)(2,1)S(1)}, bf16[256,1024]{1,0:T(8,128)(2,1)S(1)}, u32[]{:S(2)}, u32[]{:S(2)}) collective-permute-start(bf16[256,1024]{1,0:T(8,128)(2,1)S(1)} %collective-permute-done.6.refs_2_.refs_4_), channel_id=1, source_target_pairs={{1,3},{2,4},{3,5},{10,11},{11,10},{12,13},{13,12},{17,19},{18,20},... | collective-permute-start | bytes 1572872 | tf_op jit(solution)/shard_map/ppermute | solution.py:510
  35.4 1.3 %collective-permute-start.11 = (bf16[256,1024]{1,0:T(8,128)(2,1)S(1)}, bf16[256,1024]{1,0:T(8,128)(2,1)S(1)}, u32[]{:S(2)}, u32[]{:S(2)}) collective-permute-start(bf16[256,1024]{1,0:T(8,128)(2,1)S(1)} %shard_map.69.refs_0_.refs_5_), channel_id=1, source_target_pairs={{9,12},{25,28}} | collective-permute-start | bytes 1572872 | tf_op jit(solution)/shard_map/ppermute | solution.py:510
  37.3 1.3 %collective-permute-start.10 = (bf16[256,1024]{1,0:T(8,128)(2,1)S(1)}, bf16[256,1024]{1,0:T(8,128)(2,1)S(1)}, u32[]{:S(2)}, u32[]{:S(2)}) collective-permute-start(bf16[256,1024]{1,0:T(8,128)(2,1)S(1)} %shard_map.70), channel_id=1, source_target_pairs={{0,1},{2,3},{3,2},{4,5},{5,4},{6,7},{8,10},{9,11},{10,12},{11,13},... | collective-permute-start | bytes 1572872 | tf_op jit(solution)/shard_map/ppermute | solution.py:510
  38.6 6.4 %shard_map.71 = (f32[4096,256]{1,0:T(8,128)S(1)}, f32[4096,128]{1,0:T(8,128)S(1)}) custom-call(s32[22]{0:T(128)S(1)} %shard_map.64.info_ref, s32[32,128]{1,0:T(8,128)S(1)} %bitcast.3, bf16[128,1024]{1,0:T(8,128)(2,1)S(1)} %get-tuple-element.28.refs_0_, bf16[128,1024]{1,0:T(8,128)(2,1)S(1)} %collective-permute-done.refs_1_, ...), custom_call_target="tpu_custom_call" | custom-call | flops 2147483648 | bytes 2097152 | tf_op jit(solution)/shard_map/pallas_call | solution.py:376
  45.1 1.3 %collective-permute-start.13 = (bf16[256,1024]{1,0:T(8,128)(2,1)S(1)}, bf16[256,1024]{1,0:T(8,128)(2,1)S(1)}, u32[]{:S(2)}, u32[]{:S(2)}) collective-permute-start(bf16[256,1024]{1,0:T(8,128)(2,1)S(1)} %collective-permute-done.7.refs_4_), channel_id=1, source_target_pairs={{10,12},{26,28}} | collective-permute-start | bytes 1572872 | tf_op jit(solution)/shard_map/ppermute | solution.py:510
  46.4 3.5 %collective-permute-done.11.refs_7_ = bf16[256,1024]{1,0:T(8,128)(2,1)S(1)} collective-permute-done((bf16[256,1024]{1,0:T(8,128)(2,1)S(1)}, bf16[256,1024]{1,0:T(8,128)(2,1)S(1)}, u32[]{:S(2)}, u32[]{:S(2)}) %collective-permute-start.11) | collective-permute-done | bytes 524320 | tf_op jit(solution)/shard_map/ppermute | solution.py:510
  49.9 7.8 %collective-permute-start.12 = (bf16[256,1024]{1,0:T(8,128)(2,1)S(1)}, bf16[256,1024]{1,0:T(8,128)(2,1)S(1)}, u32[]{:S(2)}, u32[]{:S(2)}) collective-permute-start(bf16[256,1024]{1,0:T(8,128)(2,1)S(1)} %collective-permute-done.10.refs_5_), channel_id=1, source_target_pairs={{1,3},{2,4},{3,5},{10,11},{11,10},{12,13},{13,12},{17,19},{18,20},... | collective-permute-start | bytes 1572872 | tf_op jit(solution)/shard_map/ppermute | solution.py:510
  57.7 9.1 %shard_map.72 = (f32[4096,256]{1,0:T(8,128)S(1)}, f32[4096,128]{1,0:T(8,128)S(1)}) custom-call(s32[22]{0:T(128)S(1)} %shard_map.64.info_ref, s32[32,128]{1,0:T(8,128)S(1)} %bitcast.4, bf16[128,1024]{1,0:T(8,128)(2,1)S(1)} %get-tuple-element.28.refs_0_, ...), custom_call_target="tpu_custom_call", output_to_operand_aliasing={{0}: (10, {}), {1}: (11, {})} | custom-call | flops 2147483648 | bytes 2097152 | tf_op jit(solution)/shard_map/pallas_call | solution.py:376
  66.8 2.9 %shard_map.74 = (bf16[128,512]{1,0:T(8,128)(2,1)S(1)}, bf16[128,512]{1,0:T(8,128)(2,1)S(1)}, bf16[128,512]{1,0:T(8,128)(2,1)S(1)}, bf16[128,512]{1,0:T(8,128)(2,1)S(1)}) custom-call(s32[22]{0:T(128)S(1)} %shard_map.64.info_ref, s32[32,128]{1,0:T(8,128)S(1)} %bitcast.5, bf16[128,1024]{1,0:T(8,128)(2,1)S(1)} %get-tuple-element.28.refs_0_, ...), custom_call_target="tpu_custom_call" | custom-call | flops 536870912 | bytes 2097152 | tf_op jit(solution)/shard_map/pallas_call | solution.py:376
  69.8 1.3 %collective-permute-start.18 = (bf16[128,512]{1,0:T(8,128)(2,1)S(1)}, bf16[128,512]{1,0:T(8,128)(2,1)S(1)}, u32[]{:S(2)}, u32[]{:S(2)}) collective-permute-start(bf16[128,512]{1,0:T(8,128)(2,1)S(1)} %get-tuple-element.49), channel_id=1, source_target_pairs={{0,16},{8,24},{16,0},{24,8},{1,17},{9,25},{17,1},{25,9},{2,18},{10... | collective-permute-start | bytes 393224 | tf_op jit(solution)/shard_map/ppermute | solution.py:435
  72.0 2.7 %shard_map.73 = (bf16[128,512]{1,0:T(8,128)(2,1)S(1)}, bf16[128,512]{1,0:T(8,128)(2,1)S(1)}, bf16[128,512]{1,0:T(8,128)(2,1)S(1)}, bf16[128,512]{1,0:T(8,128)(2,1)S(1)}) custom-call(s32[22]{0:T(128)S(1)} %shard_map.64.info_ref, s32[32,128]{1,0:T(8,128)S(1)} %bitcast.6, bf16[128,1024]{1,0:T(8,128)(2,1)S(1)} %get-tuple-element.28.refs_0_, ...), custom_call_target="tpu_custom_call" | custom-call | flops 536870912 | bytes 2097152 | tf_op jit(solution)/shard_map/pallas_call | solution.py:376
  74.8 1.3 %collective-permute-start.15 = (bf16[128,512]{1,0:T(8,128)(2,1)S(1)}, bf16[128,512]{1,0:T(8,128)(2,1)S(1)}, u32[]{:S(2)}, u32[]{:S(2)}) collective-permute-start(bf16[128,512]{1,0:T(8,128)(2,1)S(1)} %get-tuple-element.45), channel_id=1, source_target_pairs={{0,16},{8,24},{16,0},{24,8},{1,17},{9,25},{17,1},{25,9},{2,18},{10... | collective-permute-start | bytes 393224 | tf_op jit(solution)/shard_map/ppermute | solution.py:435
  76.9 1.6 %collective-permute-done.19.refs_7_ = bf16[128,512]{1,0:T(8,128)(2,1)S(1)} collective-permute-done((bf16[128,512]{1,0:T(8,128)(2,1)S(1)}, bf16[128,512]{1,0:T(8,128)(2,1)S(1)}, u32[]{:S(2)}, u32[]{:S(2)}) %collective-permute-start.19) | collective-permute-done | bytes 131104 | tf_op jit(solution)/shard_map/ppermute | solution.py:435
  78.5 1.9 %collective-permute-done.15.refs_2_ = bf16[128,512]{1,0:T(8,128)(2,1)S(1)} collective-permute-done((bf16[128,512]{1,0:T(8,128)(2,1)S(1)}, bf16[128,512]{1,0:T(8,128)(2,1)S(1)}, u32[]{:S(2)}, u32[]{:S(2)}) %collective-permute-start.15) | collective-permute-done | bytes 131104 | tf_op jit(solution)/shard_map/ppermute | solution.py:435
  80.5 3.1 %collective-permute-done.16.refs_3_ = bf16[128,512]{1,0:T(8,128)(2,1)S(1)} collective-permute-done((bf16[128,512]{1,0:T(8,128)(2,1)S(1)}, bf16[128,512]{1,0:T(8,128)(2,1)S(1)}, u32[]{:S(2)}, u32[]{:S(2)}) %collective-permute-start.16) | collective-permute-done | bytes 131104 | tf_op jit(solution)/shard_map/ppermute | solution.py:435
  83.6 1.6 %shard_map.75 = bf16[128,4096]{1,0:T(8,128)(2,1)} custom-call(s32[2]{0:T(128)S(1)} %pad_add_fusion.place_ref, bf16[128,512]{1,0:T(8,128)(2,1)S(1)} %get-tuple-element.43.refs_0_, bf16[128,512]{1,0:T(8,128)(2,1)S(1)} %collective-permute-done.14.refs_1_, bf16[128,512]{1,0:T(8,128)(2,1)S(1)} %collective-permute-done.15.refs_2_, ...), custom_call_target="tpu_custom_call" | custom-call | bytes 2097152 | tf_op jit(solution)/shard_map/pallas_call | solution.py:102
  (45 shorter events, 12.8 us)
Async XLA Ops:
  0.1 1.0 %copy-start.1 = (bf16[128,2048]{1,0:T(8,128)(2,1)S(1)}, bf16[128,2048]{1,0:T(8,128)(2,1)}, u32[]{:S(2)}) copy-start(bf16[128,2048]{1,0:T(8,128)(2,1)} %refs_0_.3) | copy-start | bytes 1572868
  1.1 1.0 %copy-start.2 = (bf16[128,2048]{1,0:T(8,128)(2,1)S(1)}, bf16[128,2048]{1,0:T(8,128)(2,1)}, u32[]{:S(2)}) copy-start(bf16[128,2048]{1,0:T(8,128)(2,1)} %refs_1_.1) | copy-start | bytes 1572868
  3.0 1.9 %collective-permute-start.4 = (bf16[128,1024]{1,0:T(8,128)(2,1)S(1)}, bf16[128,1024]{1,0:T(8,128)(2,1)S(1)}, u32[]{:S(2)}, u32[]{:S(2)}) collective-permute-start(bf16[128,1024]{1,0:T(8,128)(2,1)S(1)} %get-tuple-element.34), channel_id=1, source_target_pairs={{0,8},{8,0},{16,24},{24,16},{1,9},{9,1},{17,25},{25,17},{2,10},{10... | collective-permute-start | bytes 786440 | tf_op jit(solution)/shard_map/ppermute | solution.py:435
  3.7 13.5 %collective-permute-start.1 = (bf16[256,1024]{1,0:T(8,128)(2,1)S(1)}, bf16[256,1024]{1,0:T(8,128)(2,1)S(1)}, u32[]{:S(2)}, u32[]{:S(2)}) collective-permute-start(bf16[256,1024]{1,0:T(8,128)(2,1)S(1)} %get-tuple-element.31), channel_id=1, source_target_pairs={{0,16},{8,24},{16,0},{24,8},{1,17},{9,25},{17,1},{25,9},{2,18},{10... | collective-permute-start | bytes 1572872 | tf_op jit(solution)/shard_map/ppermute | solution.py:435
  4.9 33.8 %copy-start.4 = (s32[4096]{0:T(1024)S(1)}, s32[4096]{0:T(1024)}, u32[]{:S(2)}) copy-start(s32[4096]{0:T(1024)} %doc_ref.1) | copy-start | bytes 49156
  5.5 12.9 %collective-permute-start.5 = (bf16[256,1024]{1,0:T(8,128)(2,1)S(1)}, bf16[256,1024]{1,0:T(8,128)(2,1)S(1)}, u32[]{:S(2)}, u32[]{:S(2)}) collective-permute-start(bf16[256,1024]{1,0:T(8,128)(2,1)S(1)} %shard_map.67.refs_0_.refs_4_), channel_id=1, source_target_pairs={{0,2},{1,3},{2,4},{3,5},{5,6},{8,9},{10,11},{12,13},{14,15},{16,18... | collective-permute-start | bytes 1572872 | tf_op jit(solution)/shard_map/ppermute | solution.py:510
  8.6 1.2 %copy-start = (bf16[128,4096]{1,0:T(8,128)(2,1)S(1)}, bf16[128,4096]{1,0:T(8,128)(2,1)}, u32[]{:S(2)}) copy-start(bf16[128,4096]{1,0:T(8,128)(2,1)} %refs_0_.2) | copy-start | bytes 3145732
  17.2 3.1 %collective-permute-start.8 = (bf16[128,1024]{1,0:T(8,128)(2,1)S(1)}, bf16[128,1024]{1,0:T(8,128)(2,1)S(1)}, u32[]{:S(2)}, u32[]{:S(2)}) collective-permute-start(bf16[128,1024]{1,0:T(8,128)(2,1)S(1)} %slice.7), channel_id=1, source_target_pairs={{0,8},{8,0},{16,24},{24,16},{1,9},{9,1},{17,25},{25,17},{2,10},{10... | collective-permute-start | bytes 786440 | tf_op jit(solution)/shard_map/ppermute | solution.py:435
  18.1 13.5 %collective-permute-start.2 = (bf16[256,1024]{1,0:T(8,128)(2,1)S(1)}, bf16[256,1024]{1,0:T(8,128)(2,1)S(1)}, u32[]{:S(2)}, u32[]{:S(2)}) collective-permute-start(bf16[256,1024]{1,0:T(8,128)(2,1)S(1)} %get-tuple-element.32), channel_id=1, source_target_pairs={{0,16},{8,24},{16,0},{24,8},{1,17},{9,25},{17,1},{25,9},{2,18},{10... | collective-permute-start | bytes 1572872 | tf_op jit(solution)/shard_map/ppermute | solution.py:435
  19.0 12.7 %collective-permute-start.6 = (bf16[256,1024]{1,0:T(8,128)(2,1)S(1)}, bf16[256,1024]{1,0:T(8,128)(2,1)S(1)}, u32[]{:S(2)}, u32[]{:S(2)}) collective-permute-start(bf16[256,1024]{1,0:T(8,128)(2,1)S(1)} %shard_map.68), channel_id=1, source_target_pairs={{0,1},{2,3},{3,2},{4,5},{5,4},{6,7},{8,10},{9,11},{10,12},{11,13},... | collective-permute-start | bytes 1572872 | tf_op jit(solution)/shard_map/ppermute | solution.py:510
  20.9 15.8 %collective-permute-start.9 = (bf16[256,1024]{1,0:T(8,128)(2,1)S(1)}, bf16[256,1024]{1,0:T(8,128)(2,1)S(1)}, u32[]{:S(2)}, u32[]{:S(2)}) collective-permute-start(bf16[256,1024]{1,0:T(8,128)(2,1)S(1)} %shard_map.69.refs_0_.refs_5_), channel_id=1, source_target_pairs={{0,2},{1,3},{2,4},{3,5},{5,6},{8,9},{10,11},{12,13},{14,15},{16,18... | collective-permute-start | bytes 1572872 | tf_op jit(solution)/shard_map/ppermute | solution.py:510
  31.6 13.5 %collective-permute-start.7 = (bf16[256,1024]{1,0:T(8,128)(2,1)S(1)}, bf16[256,1024]{1,0:T(8,128)(2,1)S(1)}, u32[]{:S(2)}, u32[]{:S(2)}) collective-permute-start(bf16[256,1024]{1,0:T(8,128)(2,1)S(1)} %collective-permute-done.6.refs_2_.refs_4_), channel_id=1, source_target_pairs={{1,3},{2,4},{3,5},{10,11},{11,10},{12,13},{13,12},{17,19},{18,20},... | collective-permute-start | bytes 1572872 | tf_op jit(solution)/shard_map/ppermute | solution.py:510
  34.8 3.9 %collective-permute-start = (bf16[128,1024]{1,0:T(8,128)(2,1)S(1)}, bf16[128,1024]{1,0:T(8,128)(2,1)S(1)}, u32[]{:S(2)}, u32[]{:S(2)}) collective-permute-start(bf16[128,1024]{1,0:T(8,128)(2,1)S(1)} %get-tuple-element.29), channel_id=1, source_target_pairs={{0,8},{8,0},{16,24},{24,16},{1,9},{9,1},{17,25},{25,17},{2,10},{10... | collective-permute-start | bytes 786440 | tf_op jit(solution)/shard_map/ppermute | solution.py:435
  34.9 3.8 %collective-permute-start.3 = (bf16[128,1024]{1,0:T(8,128)(2,1)S(1)}, bf16[128,1024]{1,0:T(8,128)(2,1)S(1)}, u32[]{:S(2)}, u32[]{:S(2)}) collective-permute-start(bf16[128,1024]{1,0:T(8,128)(2,1)S(1)} %slice.8), channel_id=1, source_target_pairs={{0,8},{8,0},{16,24},{24,16},{1,9},{9,1},{17,25},{25,17},{2,10},{10... | collective-permute-start | bytes 786440 | tf_op jit(solution)/shard_map/ppermute | solution.py:435
  35.4 14.4 %collective-permute-start.11 = (bf16[256,1024]{1,0:T(8,128)(2,1)S(1)}, bf16[256,1024]{1,0:T(8,128)(2,1)S(1)}, u32[]{:S(2)}, u32[]{:S(2)}) collective-permute-start(bf16[256,1024]{1,0:T(8,128)(2,1)S(1)} %shard_map.69.refs_0_.refs_5_), channel_id=1, source_target_pairs={{9,12},{25,28}} | collective-permute-start | bytes 1572872 | tf_op jit(solution)/shard_map/ppermute | solution.py:510
  37.3 12.6 %collective-permute-start.10 = (bf16[256,1024]{1,0:T(8,128)(2,1)S(1)}, bf16[256,1024]{1,0:T(8,128)(2,1)S(1)}, u32[]{:S(2)}, u32[]{:S(2)}) collective-permute-start(bf16[256,1024]{1,0:T(8,128)(2,1)S(1)} %shard_map.70), channel_id=1, source_target_pairs={{0,1},{2,3},{3,2},{4,5},{5,4},{6,7},{8,10},{9,11},{10,12},{11,13},... | collective-permute-start | bytes 1572872 | tf_op jit(solution)/shard_map/ppermute | solution.py:510
  45.1 12.6 %collective-permute-start.13 = (bf16[256,1024]{1,0:T(8,128)(2,1)S(1)}, bf16[256,1024]{1,0:T(8,128)(2,1)S(1)}, u32[]{:S(2)}, u32[]{:S(2)}) collective-permute-start(bf16[256,1024]{1,0:T(8,128)(2,1)S(1)} %collective-permute-done.7.refs_4_), channel_id=1, source_target_pairs={{10,12},{26,28}} | collective-permute-start | bytes 1572872 | tf_op jit(solution)/shard_map/ppermute | solution.py:510
  49.9 16.9 %collective-permute-start.12 = (bf16[256,1024]{1,0:T(8,128)(2,1)S(1)}, bf16[256,1024]{1,0:T(8,128)(2,1)S(1)}, u32[]{:S(2)}, u32[]{:S(2)}) collective-permute-start(bf16[256,1024]{1,0:T(8,128)(2,1)S(1)} %collective-permute-done.10.refs_5_), channel_id=1, source_target_pairs={{1,3},{2,4},{3,5},{10,11},{11,10},{12,13},{13,12},{17,19},{18,20},... | collective-permute-start | bytes 1572872 | tf_op jit(solution)/shard_map/ppermute | solution.py:510
  69.8 6.3 %collective-permute-start.17 = (bf16[128,512]{1,0:T(8,128)(2,1)S(1)}, bf16[128,512]{1,0:T(8,128)(2,1)S(1)}, u32[]{:S(2)}, u32[]{:S(2)}) collective-permute-start(bf16[128,512]{1,0:T(8,128)(2,1)S(1)} %get-tuple-element.48), channel_id=1, source_target_pairs={{0,8},{8,0},{16,24},{24,16},{1,9},{9,1},{17,25},{25,17},{2,10},{10... | collective-permute-start | bytes 393224 | tf_op jit(solution)/shard_map/ppermute | solution.py:435
  69.8 7.1 %collective-permute-start.18 = (bf16[128,512]{1,0:T(8,128)(2,1)S(1)}, bf16[128,512]{1,0:T(8,128)(2,1)S(1)}, u32[]{:S(2)}, u32[]{:S(2)}) collective-permute-start(bf16[128,512]{1,0:T(8,128)(2,1)S(1)} %get-tuple-element.49), channel_id=1, source_target_pairs={{0,16},{8,24},{16,0},{24,8},{1,17},{9,25},{17,1},{25,9},{2,18},{10... | collective-permute-start | bytes 393224 | tf_op jit(solution)/shard_map/ppermute | solution.py:435
  71.1 7.4 %collective-permute-start.19 = (bf16[128,512]{1,0:T(8,128)(2,1)S(1)}, bf16[128,512]{1,0:T(8,128)(2,1)S(1)}, u32[]{:S(2)}, u32[]{:S(2)}) collective-permute-start(bf16[128,512]{1,0:T(8,128)(2,1)S(1)} %get-tuple-element.50), channel_id=1, source_target_pairs={{0,24},{8,16},{16,8},{24,0},{1,25},{9,17},{17,9},{25,1},{2,26},{10... | collective-permute-start | bytes 393224 | tf_op jit(solution)/shard_map/ppermute | solution.py:435
  74.7 3.8 %collective-permute-start.14 = (bf16[128,512]{1,0:T(8,128)(2,1)S(1)}, bf16[128,512]{1,0:T(8,128)(2,1)S(1)}, u32[]{:S(2)}, u32[]{:S(2)}) collective-permute-start(bf16[128,512]{1,0:T(8,128)(2,1)S(1)} %get-tuple-element.44), channel_id=1, source_target_pairs={{0,8},{8,0},{16,24},{24,16},{1,9},{9,1},{17,25},{25,17},{2,10},{10... | collective-permute-start | bytes 393224 | tf_op jit(solution)/shard_map/ppermute | solution.py:435
  74.8 5.6 %collective-permute-start.15 = (bf16[128,512]{1,0:T(8,128)(2,1)S(1)}, bf16[128,512]{1,0:T(8,128)(2,1)S(1)}, u32[]{:S(2)}, u32[]{:S(2)}) collective-permute-start(bf16[128,512]{1,0:T(8,128)(2,1)S(1)} %get-tuple-element.45), channel_id=1, source_target_pairs={{0,16},{8,24},{16,0},{24,8},{1,17},{9,25},{17,1},{25,9},{2,18},{10... | collective-permute-start | bytes 393224 | tf_op jit(solution)/shard_map/ppermute | solution.py:435
  76.1 7.4 %collective-permute-start.16 = (bf16[128,512]{1,0:T(8,128)(2,1)S(1)}, bf16[128,512]{1,0:T(8,128)(2,1)S(1)}, u32[]{:S(2)}, u32[]{:S(2)}) collective-permute-start(bf16[128,512]{1,0:T(8,128)(2,1)S(1)} %get-tuple-element.46), channel_id=1, source_target_pairs={{0,24},{8,16},{16,8},{24,0},{1,25},{9,17},{17,9},{25,1},{2,26},{10... | collective-permute-start | bytes 393224 | tf_op jit(solution)/shard_map/ppermute | solution.py:435
  (2 other events, 1.4 us)

commit v3 on v2

--- a/solution.py
+++ b/solution.py
@@ -42,22 +42,20 @@
     def free(k, s, t):
         return t not in rounds[k] and all(entry[0] != s for entry in rounds[k].values())
 
-    for k in range(3):
+    for k in range(4):
         rounds.append({})
         had = [dict(x) for x in held]
         for s in range(count):
-            t = s + 2 if (k + kind) % 2 == 0 else s ^ 1
-            if t >= count:
+            t = s + 2 if k in ((0, 3) if kind == 0 else (1,)) else s ^ 1
+            if t >= count or (k == 2 and (kind == 1 or s % 2 == 0)):
                 continue
-            choice = [b for b in had[s] if b in missing(t)]
+            choice = [b for b in had[s] if b in missing(t) and (k > 1 or b == s)]
             if choice:
                 send(k, s, t, max(choice))
     for t in range(count):
         for b in missing(t):
-            options = [
-                (k, b) for k in range(3) if t - b == 1 and (k + kind) % 2 == 0 and free(k, b, t)
-            ]
-            k = 3
+            options = [(k, b) for k in (kind,) if t - b == 1 and free(k, b, t)]
+            k = 4
             while not options:
                 if k == len(rounds):
                     rounds.append({})
@@ -77,12 +75,12 @@
 in_hbm = pl.BlockSpec(memory_space=pltpu.HBM)
 
 
-def move(place, operands, copies, shapes, source_spec, target_spec, after=(), weight=1):
+def move(place, operands, copies, shapes, source_spec, target_spec, after=(), into=()):
     count_in = len(operands)
 
     def kernel(place_ref, *refs):
         h = place_ref[1]
-        sources, targets, sems = refs[:count_in], refs[count_in + len(after) : -1], refs[-1]
+        sources, targets, sems = refs[:count_in], refs[-1 - len(shapes) : -1], refs[-1]
 
         def span(value, size):
             return pl.ds(pl.multiple_of(value(h), 128) if callable(value) else value, size)
@@ -102,18 +100,22 @@
     return pl.pallas_call(
         kernel,
         out_shape=[jax.ShapeDtypeStruct(s, jnp.bfloat16) for s in shapes],
-        in_specs=[in_smem] + [source_spec] * count_in + [anywhere] * len(after),
+        in_specs=[in_smem]
+        + [source_spec] * count_in
+        + [anywhere] * len(after)
+        + [target_spec] * len(into),
         out_specs=[target_spec] * len(shapes),
+        input_output_aliases={1 + count_in + len(after) + i: i for i in range(len(into))},
         scratch_shapes=[pltpu.SemaphoreType.DMA((len(copies),))],
         compiler_params=pltpu.CompilerParams(
             vmem_limit_bytes=SMALL_VMEM
         ),
         cost_estimate=pl.CostEstimate(
             flops=0,
-            bytes_accessed=weight * sum(4 * c[2] * c[4] for c in copies),
+            bytes_accessed=sum(4 * c[2] * c[4] for c in copies),
             transcendentals=0,
         ),
-    )(place, *operands, *after)
+    )(place, *operands, *after, *into)
 
 
 def survey(place, table, documents, readers, entries, rounds, window, slots, rows):
@@ -129,7 +131,7 @@
             k_first, k_last = doc_ref[block * rows], doc_ref[block * rows + rows - 1]
             distance = jnp.clip(ctx - block, 0, window - 1)
             live = (
-                (number >= 0) & (read_ref[block * window + distance] > 0) & (k_last == q_first)
+                (number >= 0) & (read_ref[distance, block] > 0) & (k_last == q_first)
             )
             out_ref[2 + 3 * k] = block
             out_ref[3 + 3 * k] = live.astype(jnp.int32)
@@ -245,7 +247,7 @@
                 row += size
 
         def give(n, r, sums):
-            out_refs[r][:, lanes_of(n - heads[0] * GROUP)] = (
+            out_refs[final.index(r)][:, lanes_of(n - heads[0] * GROUP)] = (
                 sums[:, :HEAD_WIDTH] / sums[:, HEAD_WIDTH:]
             ).astype(jnp.bfloat16)
 
@@ -301,7 +303,7 @@
             def work(kv_head):
                 load(index, kv_head)
                 for g in range(GROUP):
-                    for r in range(slots):
+                    for r in final or range(slots):
                         tile(kv_head * GROUP + g, r, 0, rows, masked, first)
 
             each_head(work)
@@ -334,7 +336,11 @@
             if slot == 0:
                 run_own()
                 continue
+            slot, *guard = slot if isinstance(slot, tuple) else (slot,)
             block, live, full = [info_ref[3 * slot - 1 + i] for i in range(3)]
+            if guard:
+                other = info_ref[3 * guard[0]]
+                live = jnp.where((other != 0) == guard[1], live, 0)
 
             @pl.when((live != 0) & (full != 0))
             def _(index=index):
@@ -351,7 +357,7 @@
                 def _():
                     def work(kv_head):
                         for n in (kv_head * GROUP + g for g in range(GROUP)):
-                            for r in range(slots):
+                            for r in final:
                                 give(n, r, acc[rows_of(n, r), :])
 
                     each_head(work)
@@ -365,7 +371,7 @@
     if final:
         out_shape = [
             jax.ShapeDtypeStruct((tokens, len(heads) * GROUP * HEAD_WIDTH), jnp.bfloat16)
-        ] * slots
+        ] * len(final)
     else:
         out_shape = [
             jax.ShapeDtypeStruct((stacked, 2 * HEAD_WIDTH), jnp.float32),
@@ -387,7 +393,7 @@
         ],
         compiler_params=pltpu.CompilerParams(vmem_limit_bytes=SMALL_VMEM + scratch),
         cost_estimate=pl.CostEstimate(
-            flops=4 * scores_made * HEAD_WIDTH,
+            flops=2 * scores_made * HEAD_WIDTH,
             bytes_accessed=4 * stacked * HEAD_WIDTH,
             transcendentals=scores_made,
         ),
@@ -427,7 +433,7 @@
                     sends = [e[2] for e in plan[h % 2][k].values() if e[0] == c]
                     table.append(sends[0] if sends else -1)
     info = survey(
-        place, jnp.array(table, jnp.int32), documents, readers.reshape(-1), entries, length, window,
+        place, jnp.array(table, jnp.int32), documents, readers.T, entries, length, window,
         slots, slots * tokens,
     )
 
@@ -510,9 +516,10 @@
         held[part][k + 1] = lax.ppermute(operand, ("head", "ctx"), pairs)
         return operand
 
-    def attended(heads, chosen, state, final=False):
+    def attended(heads, chosen, state, final=None):
         asked = [queries[r] for r in range(slots)]
-        blocks = [[part[slot] for part in held] for slot in chosen]
+        plain = [slot[0] if isinstance(slot, tuple) else slot for slot in chosen]
+        blocks = [[part[slot] for part in held] for slot in plain]
         return attend(info, doc_rows, asked, heads, blocks, chosen, state, final)
 
     halves = [range(key_heads)]
@@ -522,53 +529,64 @@
     spots = exchanged([key_matrix, value_matrix], [local_keys] * 2)
     held = [{0: part_of(spots, groups[0])}]
     send(0, 0)
-    send(0, 1)
+    send(0, 1, [info])
     across = range(2, slots, 2)
     queries = exchanged([query_matrix], [local_queries], [spots[r][0] for r in across])
     arrived = [queries[r][0] for r in across]
-    shared(spots, [queries[0][0], info])
+    shared(spots, [queries[0][0]])
     for part in later:
-        held.append({0: part_of(spots, groups[part], [held[0][1]])})
+        held.append({0: part_of(spots, groups[part], [held[0][1], held[0][2]])})
         send(part, 0)
+        send(part, 1)
     shared(queries)
-    send(0, 2, arrived)
+    send(0, 2)
+    state = attended(range(key_heads), [0], None)
+    send(0, 3, arrived)
+    more = range(4, length)
     for part in later:
-        send(part, 1, [held[0][2]])
-        for k in range(3, length):
+        for k in more:
             send(part, k)
-    state = attended(range(key_heads), [0, 1], None)
-    for k in range(3, length):
+        send(part, 2, [held[part][2], state[1]] + [held[part][k + 1] for k in more])
+    state = attended(range(key_heads), [1, (2, 1, False)], state)
+    for k in more:
         send(0, k, [state[1]])
     for part in later:
-        extra = [held[part][k + 1] for k in range(3, length)]
-        send(part, 2, [held[0][3]] + extra + [state[1]])
-    state = attended(range(key_heads), [2] + list(range(4, length + 1)), state)
+        send(part, 3, [held[0][4], state[1]])
+    state = attended(
+        range(key_heads), [(2, 1, True), 3] + [k + 1 for k in more], state
+    )
     results = []
+    others = list(range(1, slots))
     for heads in halves:
-        outs = attended(heads, [3], state, True)
-        results += [swap(outs[r], r) if r else outs[r] for r in range(slots)]
-    half_queries = local_queries // len(halves)
-    return move(
-        place,
-        results,
-        [
-            (
-                number * slots + r,
-                0,
-                tokens,
-                0,
-                half_queries,
-                0,
-                0,
-                lambda h, r=r, number=number: (h ^ r) * local_queries + number * half_queries,
-            )
-            for number in range(len(halves))
-            for r in range(slots)
-        ],
-        [query_matrix.shape],
-        in_vmem,
-        anywhere,
-    )[0]
+        outs = attended(heads, [4], state, others)
+        results.append([(swap(out, r), r, heads[0]) for r, out in zip(others, outs)])
+    results[0].append((attended(range(key_heads), [4], state, [0])[0], 0, 0))
+    whole = ()
+    for group in results:
+        whole = move(
+            place,
+            [out for out, _, _ in group],
+            [
+                (
+                    number,
+                    0,
+                    tokens,
+                    0,
+                    out.shape[1],
+                    0,
+                    0,
+                    lambda h, r=r, first=first: (h ^ r) * local_queries
+                    + first * GROUP * HEAD_WIDTH,
+                )
+                for number, (out, r, first) in enumerate(group)
+            ],
+            [query_matrix.shape],
+            in_vmem,
+            anywhere,
+            (),
+            whole,
+        )
+    return whole[0]
 
 
 def solution(mesh):

time: 86.8 us -> 85.5 us (0.985); the launches traced: 85.3 us -> 85 us
  waiting for transfers between devices: 19.7 us -> 12.5 us
  Pallas kernels: 28.2 us -> 32.1 us
  starting transfers between devices: 31.4 us -> 34.5 us
    ppermute x12, waiting for transfers between devices: 16.2 us -> 7.19 us  [swap(): return lax.ppermute(value, 'head', [(h, h ^ r) for h in range(slots)])]
    ppermute x12, starting transfers between devices: 7.16 us -> 13.3 us  [swap(): return lax.ppermute(value, 'head', [(h, h ^ r) for h in range(slots)])]
    ppermute x8 -> x10, starting transfers between devices: 24.2 us -> 21.2 us  [send(): held[part][k + 1] = lax.ppermute(operand, ('head', 'ctx'), pairs)]
    pallas_call x4 -> x6, Pallas kernels: 21.3 us -> 24 us  [attend(): pl.pallas_call(kernel, out_shape=out_shape, in_specs=[in_smem] + [in_vmem...]
    ppermute x8 -> x10, waiting for transfers between devices: 3.47 us -> 5.28 us  [send(): held[part][k + 1] = lax.ppermute(operand, ('head', 'ctx'), pairs)]
    pallas_call x5 -> x6, Pallas kernels: 4.25 us -> 5.41 us  [move(): pl.pallas_call(kernel, out_shape=[jax.ShapeDtypeStruct(s, jnp.bfloat16) f...]
    unnamed x13 -> x14, local copies, waits for them, and re-layouts: 5.47 us -> 5.38 us
  transfers between devices with their start and end apart: 20 -> 22, of which waited for: 7 -> 8; matrix products, arithmetic and copies ran while one was open for 1% -> 0% of each run, Pallas kernels for 27% -> 32%
where the time goes in v3:
time: 85.5 us; the launch traced here: 85 us
  starting transfers between devices  34.5 us (40%)
  Pallas kernels  32.1 us (38%)
  waiting for transfers between devices  12.5 us (15%)
  local copies, waits for them, and re-layouts  5.42 us (6%)
    pallas_call x6, Pallas kernels, attend(): pl.pallas_call(kernel, out_shape=out_shape, in_specs=[in_smem] + [in_vmem...  24 us
    ppermute x10, starting transfers between devices, send(): held[part][k + 1] = lax.ppermute(operand, ('head', 'ctx'), pairs)  21.2 us
    ppermute x12, starting transfers between devices, swap(): return lax.ppermute(value, 'head', [(h, h ^ r) for h in range(slots)])  13.3 us
    ppermute x12, waiting for transfers between devices, swap(): return lax.ppermute(value, 'head', [(h, h ^ r) for h in range(slots)])  7.19 us
    pallas_call x6, Pallas kernels, move(): pl.pallas_call(kernel, out_shape=[jax.ShapeDtypeStruct(s, jnp.bfloat16) f...  5.41 us
    unnamed x14, local copies, waits for them, and re-layouts  5.38 us
    ppermute x10, waiting for transfers between devices, send(): held[part][k + 1] = lax.ppermute(operand, ('head', 'ctx'), pairs)  5.28 us
  transfers between devices with their start and end apart: 22, of which 8 were waited for; matrix products, arithmetic and copies ran while one was open for 0% of the time, Pallas kernels for 32%

profile of v3, /device:TPU:21, one launch (start us, length us, event | category | flops | bytes accessed | tf_op | source)
XLA Modules:
  0.0 85.0 jit_solution(8093443650746421523)
XLA Ops:
  5.5 3.1 %collective-permute-start.6 = (bf16[256,1024]{1,0:T(8,128)(2,1)S(1)}, bf16[256,1024]{1,0:T(8,128)(2,1)S(1)}, u32[]{:S(2)}, u32[]{:S(2)}) collective-permute-start(bf16[256,1024]{1,0:T(8,128)(2,1)S(1)} %shard_map.67.refs_4_), channel_id=1, source_target_pairs={{0,2},{1,3},{2,4},{3,5},{5,6},{8,9},{10,11},{12,13},{14,15},{16,18... | collective-permute-start | bytes 1572872 | tf_op jit(solution)/shard_map/ppermute | solution.py:516
  10.7 1.5 %shard_map.64.info_ref = s32[27]{0:T(128)S(1)} custom-call(s32[2]{0:T(128)S(1)} %pad_add_fusion.place_ref, s32[480]{0:T(512)S(1)} %copy-done.6, s32[4096]{0:T(1024)S(1)} %copy-done.3, s32[4,8]{1,0:T(4,128)S(1)} %bitcast.10), custom_call_target="tpu_custom_call" | custom-call | tf_op jit(solution)/shard_map/pallas_call | solution.py:142
  15.5 1.7 %collective-permute-done.1.refs_0_ = bf16[256,1024]{1,0:T(8,128)(2,1)S(1)} collective-permute-done((bf16[256,1024]{1,0:T(8,128)(2,1)S(1)}, bf16[256,1024]{1,0:T(8,128)(2,1)S(1)}, u32[]{:S(2)}, u32[]{:S(2)}) %collective-permute-start.1) | collective-permute-done | bytes 524320 | tf_op jit(solution)/shard_map/ppermute | solution.py:441
  18.2 2.2 %collective-permute-start.9 = (bf16[128,1024]{1,0:T(8,128)(2,1)S(1)}, bf16[128,1024]{1,0:T(8,128)(2,1)S(1)}, u32[]{:S(2)}, u32[]{:S(2)}) collective-permute-start(bf16[128,1024]{1,0:T(8,128)(2,1)S(1)} %slice.7), channel_id=1, source_target_pairs={{0,8},{8,0},{16,24},{24,16},{1,9},{9,1},{17,25},{25,17},{2,10},{10... | collective-permute-start | bytes 786440 | tf_op jit(solution)/shard_map/ppermute | solution.py:441
  20.3 2.2 %collective-permute-done.5.refs_0_.refs_3_.refs_6_.refs_4_ = bf16[256,1024]{1,0:T(8,128)(2,1)S(1)} collective-permute-done((bf16[256,1024]{1,0:T(8,128)(2,1)S(1)}, bf16[256,1024]{1,0:T(8,128)(2,1)S(1)}, u32[]{:S(2)}, u32[]{:S(2)}) %collective-permute-start.5) | collective-permute-done | bytes 524320 | tf_op jit(solution)/shard_map/ppermute | solution.py:516
  23.1 1.3 %collective-permute-start.12 = (bf16[256,1024]{1,0:T(8,128)(2,1)S(1)}, bf16[256,1024]{1,0:T(8,128)(2,1)S(1)}, u32[]{:S(2)}, u32[]{:S(2)}) collective-permute-start(bf16[256,1024]{1,0:T(8,128)(2,1)S(1)} %shard_map.69.refs_5_), channel_id=1, source_target_pairs={{9,12},{25,28}} | collective-permute-start | bytes 1572872 | tf_op jit(solution)/shard_map/ppermute | solution.py:516
  24.4 2.7 %collective-permute-start.11 = (bf16[256,1024]{1,0:T(8,128)(2,1)S(1)}, bf16[256,1024]{1,0:T(8,128)(2,1)S(1)}, u32[]{:S(2)}, u32[]{:S(2)}) collective-permute-start(bf16[256,1024]{1,0:T(8,128)(2,1)S(1)} %shard_map.69.refs_5_), channel_id=1, source_target_pairs={{0,2},{1,3},{2,4},{3,5},{5,6},{8,9},{10,11},{12,13},{14,15},{16,18... | collective-permute-start | bytes 1572872 | tf_op jit(solution)/shard_map/ppermute | solution.py:516
  29.5 2.1 %collective-permute-start = (bf16[128,1024]{1,0:T(8,128)(2,1)S(1)}, bf16[128,1024]{1,0:T(8,128)(2,1)S(1)}, u32[]{:S(2)}, u32[]{:S(2)}) collective-permute-start(bf16[128,1024]{1,0:T(8,128)(2,1)S(1)} %get-tuple-element.29), channel_id=1, source_target_pairs={{0,8},{8,0},{16,24},{24,16},{1,9},{9,1},{17,25},{25,17},{2,10},{10... | collective-permute-start | bytes 786440 | tf_op jit(solution)/shard_map/ppermute | solution.py:441
  32.7 3.3 %collective-permute-start.8 = (bf16[256,1024]{1,0:T(8,128)(2,1)S(1)}, bf16[256,1024]{1,0:T(8,128)(2,1)S(1)}, u32[]{:S(2)}, u32[]{:S(2)}) collective-permute-start(bf16[256,1024]{1,0:T(8,128)(2,1)S(1)} %shard_map.68), channel_id=1, source_target_pairs={{1,3},{2,4},{3,5},{10,11},{11,10},{12,13},{13,12},{17,19},{18,20},... | collective-permute-start | bytes 1572872 | tf_op jit(solution)/shard_map/ppermute | solution.py:516
  36.1 6.4 %shard_map.70 = (f32[4096,256]{1,0:T(8,128)S(1)}, f32[4096,128]{1,0:T(8,128)S(1)}) custom-call(s32[27]{0:T(128)S(1)} %shard_map.64.info_ref, s32[32,128]{1,0:T(8,128)S(1)} %bitcast.4, bf16[128,1024]{1,0:T(8,128)(2,1)S(1)} %get-tuple-element.28.refs_0_, bf16[128,1024]{1,0:T(8,128)(2,1)S(1)} %collective-permute-done.refs_1_, ...), custom_call_target="tpu_custom_call" | custom-call | flops 536870912 | bytes 2097152 | tf_op jit(solution)/shard_map/pallas_call | solution.py:382
  43.7 4.9 %shard_map.71 = (f32[4096,256]{1,0:T(8,128)S(1)}, f32[4096,128]{1,0:T(8,128)S(1)}) custom-call(s32[27]{0:T(128)S(1)} %shard_map.64.info_ref, s32[32,128]{1,0:T(8,128)S(1)} %bitcast.5, bf16[128,1024]{1,0:T(8,128)(2,1)S(1)} %get-tuple-element.28.refs_0_, ...), custom_call_target="tpu_custom_call", output_to_operand_aliasing={{0}: (10, {}), {1}: (11, {})} | custom-call | flops 1073741824 | bytes 2097152 | tf_op jit(solution)/shard_map/pallas_call | solution.py:382
  48.6 1.3 %collective-permute-start.15 = (bf16[256,1024]{1,0:T(8,128)(2,1)S(1)}, bf16[256,1024]{1,0:T(8,128)(2,1)S(1)}, u32[]{:S(2)}, u32[]{:S(2)}) collective-permute-start(bf16[256,1024]{1,0:T(8,128)(2,1)S(1)} %collective-permute-done.8.refs_2_.refs_4_), channel_id=1, source_target_pairs={{10,12},{26,28}} | collective-permute-start | bytes 1572872 | tf_op jit(solution)/shard_map/ppermute | solution.py:516
  50.5 5.4 %collective-permute-start.14 = (bf16[256,1024]{1,0:T(8,128)(2,1)S(1)}, bf16[256,1024]{1,0:T(8,128)(2,1)S(1)}, u32[]{:S(2)}, u32[]{:S(2)}) collective-permute-start(bf16[256,1024]{1,0:T(8,128)(2,1)S(1)} %shard_map.72), channel_id=1, source_target_pairs={{1,3},{2,4},{3,5},{10,11},{11,10},{12,13},{13,12},{17,19},{18,20},... | collective-permute-start | bytes 1572872 | tf_op jit(solution)/shard_map/ppermute | solution.py:516
  55.9 2.6 %collective-permute-done.15.refs_8_ = bf16[256,1024]{1,0:T(8,128)(2,1)S(1)} collective-permute-done((bf16[256,1024]{1,0:T(8,128)(2,1)S(1)}, bf16[256,1024]{1,0:T(8,128)(2,1)S(1)}, u32[]{:S(2)}, u32[]{:S(2)}) %collective-permute-start.15) | collective-permute-done | bytes 524320 | tf_op jit(solution)/shard_map/ppermute | solution.py:516
  58.5 5.0 %shard_map.73 = (f32[4096,256]{1,0:T(8,128)S(1)}, f32[4096,128]{1,0:T(8,128)S(1)}) custom-call(s32[27]{0:T(128)S(1)} %shard_map.64.info_ref, s32[32,128]{1,0:T(8,128)S(1)} %bitcast.6, bf16[128,1024]{1,0:T(8,128)(2,1)S(1)} %get-tuple-element.28.refs_0_, ...), custom_call_target="tpu_custom_call", output_to_operand_aliasing={{0}: (12, {}), {1}: (13, {})} | custom-call | flops 1610612736 | bytes 2097152 | tf_op jit(solution)/shard_map/pallas_call | solution.py:382
  63.6 2.4 %shard_map.75 = (bf16[128,512]{1,0:T(8,128)(2,1)S(1)}, bf16[128,512]{1,0:T(8,128)(2,1)S(1)}, bf16[128,512]{1,0:T(8,128)(2,1)S(1)}) custom-call(s32[27]{0:T(128)S(1)} %shard_map.64.info_ref, s32[32,128]{1,0:T(8,128)S(1)} %bitcast.7, bf16[128,1024]{1,0:T(8,128)(2,1)S(1)} %get-tuple-element.28.refs_0_, bf16[128,1024]{1,0:T(8,128)(2,1)S(1)} %collective-permute-done.refs_1_, ...), custom_call_target="tpu_custom_call" | custom-call | flops 268435456 | bytes 2097152 | tf_op jit(solution)/shard_map/pallas_call | solution.py:382
  66.0 3.9 %collective-permute-start.19 = (bf16[128,512]{1,0:T(8,128)(2,1)S(1)}, bf16[128,512]{1,0:T(8,128)(2,1)S(1)}, u32[]{:S(2)}, u32[]{:S(2)}) collective-permute-start(bf16[128,512]{1,0:T(8,128)(2,1)S(1)} %get-tuple-element.48), channel_id=1, source_target_pairs={{0,8},{8,0},{16,24},{24,16},{1,9},{9,1},{17,25},{25,17},{2,10},{10... | collective-permute-start | bytes 393224 | tf_op jit(solution)/shard_map/ppermute | solution.py:441
  70.1 1.5 %collective-permute-start.21 = (bf16[128,512]{1,0:T(8,128)(2,1)S(1)}, bf16[128,512]{1,0:T(8,128)(2,1)S(1)}, u32[]{:S(2)}, u32[]{:S(2)}) collective-permute-start(bf16[128,512]{1,0:T(8,128)(2,1)S(1)} %get-tuple-element.50), channel_id=1, source_target_pairs={{0,24},{8,16},{16,8},{24,0},{1,25},{9,17},{17,9},{25,1},{2,26},{10... | collective-permute-start | bytes 393224 | tf_op jit(solution)/shard_map/ppermute | solution.py:441
  71.6 2.4 %shard_map.74 = (bf16[128,512]{1,0:T(8,128)(2,1)S(1)}, bf16[128,512]{1,0:T(8,128)(2,1)S(1)}, bf16[128,512]{1,0:T(8,128)(2,1)S(1)}) custom-call(s32[27]{0:T(128)S(1)} %shard_map.64.info_ref, s32[32,128]{1,0:T(8,128)S(1)} %bitcast.8, bf16[128,1024]{1,0:T(8,128)(2,1)S(1)} %get-tuple-element.28.refs_0_, bf16[128,1024]{1,0:T(8,128)(2,1)S(1)} %collective-permute-done.refs_1_, ...), custom_call_target="tpu_custom_call" | custom-call | flops 268435456 | bytes 2097152 | tf_op jit(solution)/shard_map/pallas_call | solution.py:382
  74.4 1.8 %collective-permute-start.18 = (bf16[128,512]{1,0:T(8,128)(2,1)S(1)}, bf16[128,512]{1,0:T(8,128)(2,1)S(1)}, u32[]{:S(2)}, u32[]{:S(2)}) collective-permute-start(bf16[128,512]{1,0:T(8,128)(2,1)S(1)} %get-tuple-element.47), channel_id=1, source_target_pairs={{0,24},{8,16},{16,8},{24,0},{1,25},{9,17},{17,9},{25,1},{2,26},{10... | collective-permute-start | bytes 393224 | tf_op jit(solution)/shard_map/ppermute | solution.py:441
  76.2 2.9 %shard_map.76.refs_3_ = bf16[128,1024]{1,0:T(8,128)(2,1)S(1)} custom-call(s32[27]{0:T(128)S(1)} %shard_map.64.info_ref, s32[32,128]{1,0:T(8,128)S(1)} %bitcast.9, bf16[128,1024]{1,0:T(8,128)(2,1)S(1)} %get-tuple-element.28.refs_0_, bf16[128,1024]{1,0:T(8,128)(2,1)S(1)} %collective-permute-done.refs_1_, bf16[256,1024]{1,0:T(8,128)(2,1)S(1)} %collective-permute-done.2.refs_2_, ...), custom_call_target="tpu_custom_call" | custom-call | flops 536870912 | bytes 2097152 | tf_op jit(solution)/shard_map/pallas_call | solution.py:382
  79.1 1.4 %shard_map.77.refs_3_ = bf16[128,4096]{1,0:T(8,128)(2,1)} custom-call(s32[2]{0:T(128)S(1)} %pad_add_fusion.place_ref, bf16[128,512]{1,0:T(8,128)(2,1)S(1)} %collective-permute-done.19.refs_0_, bf16[128,512]{1,0:T(8,128)(2,1)S(1)} %collective-permute-done.20.refs_1_, bf16[128,512]{1,0:T(8,128)(2,1)S(1)} %collective-permute-done.21.refs_2_, ...), custom_call_target="tpu_custom_call" | custom-call | bytes 1310720 | tf_op jit(solution)/shard_map/pallas_call | solution.py:100
  80.6 3.0 %collective-permute-done.18.refs_2_ = bf16[128,512]{1,0:T(8,128)(2,1)S(1)} collective-permute-done((bf16[128,512]{1,0:T(8,128)(2,1)S(1)}, bf16[128,512]{1,0:T(8,128)(2,1)S(1)}, u32[]{:S(2)}, u32[]{:S(2)}) %collective-permute-start.18) | collective-permute-done | bytes 131104 | tf_op jit(solution)/shard_map/ppermute | solution.py:441
  83.6 1.3 %shard_map.78 = bf16[128,4096]{1,0:T(8,128)(2,1)} custom-call(s32[2]{0:T(128)S(1)} %pad_add_fusion.place_ref, bf16[128,512]{1,0:T(8,128)(2,1)S(1)} %collective-permute-done.16.refs_0_, bf16[128,512]{1,0:T(8,128)(2,1)S(1)} %collective-permute-done.17.refs_1_, bf16[128,512]{1,0:T(8,128)(2,1)S(1)} %collective-permute-done.18.refs_2_, ...), custom_call_target="tpu_custom_call", output_to_operand_aliasing={{}: (4, {})} | custom-call | bytes 786432 | tf_op jit(solution)/shard_map/pallas_call | solution.py:100
  (52 shorter events, 18.2 us)
Async XLA Ops:
  2.2 33.9 %copy-start.4 = (s32[4096]{0:T(1024)S(1)}, s32[4096]{0:T(1024)}, u32[]{:S(2)}) copy-start(s32[4096]{0:T(1024)} %doc_ref.1) | copy-start | bytes 49156
  3.0 1.9 %collective-permute-start.4 = (bf16[128,1024]{1,0:T(8,128)(2,1)S(1)}, bf16[128,1024]{1,0:T(8,128)(2,1)S(1)}, u32[]{:S(2)}, u32[]{:S(2)}) collective-permute-start(bf16[128,1024]{1,0:T(8,128)(2,1)S(1)} %get-tuple-element.34), channel_id=1, source_target_pairs={{0,8},{8,0},{16,24},{24,16},{1,9},{9,1},{17,25},{25,17},{2,10},{10... | collective-permute-start | bytes 786440 | tf_op jit(solution)/shard_map/ppermute | solution.py:441
  3.7 13.5 %collective-permute-start.1 = (bf16[256,1024]{1,0:T(8,128)(2,1)S(1)}, bf16[256,1024]{1,0:T(8,128)(2,1)S(1)}, u32[]{:S(2)}, u32[]{:S(2)}) collective-permute-start(bf16[256,1024]{1,0:T(8,128)(2,1)S(1)} %get-tuple-element.31), channel_id=1, source_target_pairs={{0,16},{8,24},{16,0},{24,8},{1,17},{9,25},{17,1},{25,9},{2,18},{10... | collective-permute-start | bytes 1572872 | tf_op jit(solution)/shard_map/ppermute | solution.py:441
  5.5 12.0 %collective-permute-start.6 = (bf16[256,1024]{1,0:T(8,128)(2,1)S(1)}, bf16[256,1024]{1,0:T(8,128)(2,1)S(1)}, u32[]{:S(2)}, u32[]{:S(2)}) collective-permute-start(bf16[256,1024]{1,0:T(8,128)(2,1)S(1)} %shard_map.67.refs_4_), channel_id=1, source_target_pairs={{0,2},{1,3},{2,4},{3,5},{5,6},{8,9},{10,11},{12,13},{14,15},{16,18... | collective-permute-start | bytes 1572872 | tf_op jit(solution)/shard_map/ppermute | solution.py:516
  12.3 10.2 %collective-permute-start.5 = (bf16[256,1024]{1,0:T(8,128)(2,1)S(1)}, bf16[256,1024]{1,0:T(8,128)(2,1)S(1)}, u32[]{:S(2)}, u32[]{:S(2)}) collective-permute-start(bf16[256,1024]{1,0:T(8,128)(2,1)S(1)} %shard_map.67.refs_4_), channel_id=1, source_target_pairs={{0,1},{2,3},{4,5},{6,7},{8,10},{9,11},{10,12},{11,13},{13,14},{16,... | collective-permute-start | bytes 1572872 | tf_op jit(solution)/shard_map/ppermute | solution.py:516
  13.6 1.2 %copy-start = (bf16[128,4096]{1,0:T(8,128)(2,1)S(1)}, bf16[128,4096]{1,0:T(8,128)(2,1)}, u32[]{:S(2)}) copy-start(bf16[128,4096]{1,0:T(8,128)(2,1)} %refs_0_.2) | copy-start | bytes 3145732
  17.2 12.3 %collective-permute-start.2 = (bf16[256,1024]{1,0:T(8,128)(2,1)S(1)}, bf16[256,1024]{1,0:T(8,128)(2,1)S(1)}, u32[]{:S(2)}, u32[]{:S(2)}) collective-permute-start(bf16[256,1024]{1,0:T(8,128)(2,1)S(1)} %get-tuple-element.32), channel_id=1, source_target_pairs={{0,16},{8,24},{16,0},{24,8},{1,17},{9,25},{17,1},{25,9},{2,18},{10... | collective-permute-start | bytes 1572872 | tf_op jit(solution)/shard_map/ppermute | solution.py:441
  17.4 14.1 %collective-permute-start.7 = (bf16[256,1024]{1,0:T(8,128)(2,1)S(1)}, bf16[256,1024]{1,0:T(8,128)(2,1)S(1)}, u32[]{:S(2)}, u32[]{:S(2)}) collective-permute-start(bf16[256,1024]{1,0:T(8,128)(2,1)S(1)} %collective-permute-done.6.refs_2_.refs_4_), channel_id=1, source_target_pairs={{3,2},{5,4},{19,18},{21,20}} | collective-permute-start | bytes 1572872 | tf_op jit(solution)/shard_map/ppermute | solution.py:516
  18.2 4.3 %collective-permute-start.9 = (bf16[128,1024]{1,0:T(8,128)(2,1)S(1)}, bf16[128,1024]{1,0:T(8,128)(2,1)S(1)}, u32[]{:S(2)}, u32[]{:S(2)}) collective-permute-start(bf16[128,1024]{1,0:T(8,128)(2,1)S(1)} %slice.7), channel_id=1, source_target_pairs={{0,8},{8,0},{16,24},{24,16},{1,9},{9,1},{17,25},{25,17},{2,10},{10... | collective-permute-start | bytes 786440 | tf_op jit(solution)/shard_map/ppermute | solution.py:441
  23.1 19.4 %collective-permute-start.12 = (bf16[256,1024]{1,0:T(8,128)(2,1)S(1)}, bf16[256,1024]{1,0:T(8,128)(2,1)S(1)}, u32[]{:S(2)}, u32[]{:S(2)}) collective-permute-start(bf16[256,1024]{1,0:T(8,128)(2,1)S(1)} %shard_map.69.refs_5_), channel_id=1, source_target_pairs={{9,12},{25,28}} | collective-permute-start | bytes 1572872 | tf_op jit(solution)/shard_map/ppermute | solution.py:516
  24.4 18.1 %collective-permute-start.11 = (bf16[256,1024]{1,0:T(8,128)(2,1)S(1)}, bf16[256,1024]{1,0:T(8,128)(2,1)S(1)}, u32[]{:S(2)}, u32[]{:S(2)}) collective-permute-start(bf16[256,1024]{1,0:T(8,128)(2,1)S(1)} %shard_map.69.refs_5_), channel_id=1, source_target_pairs={{0,2},{1,3},{2,4},{3,5},{5,6},{8,9},{10,11},{12,13},{14,15},{16,18... | collective-permute-start | bytes 1572872 | tf_op jit(solution)/shard_map/ppermute | solution.py:516
  27.1 15.9 %collective-permute-start.10 = (bf16[256,1024]{1,0:T(8,128)(2,1)S(1)}, bf16[256,1024]{1,0:T(8,128)(2,1)S(1)}, u32[]{:S(2)}, u32[]{:S(2)}) collective-permute-start(bf16[256,1024]{1,0:T(8,128)(2,1)S(1)} %shard_map.69.refs_5_), channel_id=1, source_target_pairs={{0,1},{2,3},{4,5},{6,7},{8,10},{9,11},{10,12},{11,13},{13,14},{16,... | collective-permute-start | bytes 1572872 | tf_op jit(solution)/shard_map/ppermute | solution.py:516
  29.5 3.2 %collective-permute-start = (bf16[128,1024]{1,0:T(8,128)(2,1)S(1)}, bf16[128,1024]{1,0:T(8,128)(2,1)S(1)}, u32[]{:S(2)}, u32[]{:S(2)}) collective-permute-start(bf16[128,1024]{1,0:T(8,128)(2,1)S(1)} %get-tuple-element.29), channel_id=1, source_target_pairs={{0,8},{8,0},{16,24},{24,16},{1,9},{9,1},{17,25},{25,17},{2,10},{10... | collective-permute-start | bytes 786440 | tf_op jit(solution)/shard_map/ppermute | solution.py:441
  31.6 4.5 %collective-permute-start.3 = (bf16[128,1024]{1,0:T(8,128)(2,1)S(1)}, bf16[128,1024]{1,0:T(8,128)(2,1)S(1)}, u32[]{:S(2)}, u32[]{:S(2)}) collective-permute-start(bf16[128,1024]{1,0:T(8,128)(2,1)S(1)} %slice.8), channel_id=1, source_target_pairs={{0,8},{8,0},{16,24},{24,16},{1,9},{9,1},{17,25},{25,17},{2,10},{10... | collective-permute-start | bytes 786440 | tf_op jit(solution)/shard_map/ppermute | solution.py:441
  32.7 15.9 %collective-permute-start.8 = (bf16[256,1024]{1,0:T(8,128)(2,1)S(1)}, bf16[256,1024]{1,0:T(8,128)(2,1)S(1)}, u32[]{:S(2)}, u32[]{:S(2)}) collective-permute-start(bf16[256,1024]{1,0:T(8,128)(2,1)S(1)} %shard_map.68), channel_id=1, source_target_pairs={{1,3},{2,4},{3,5},{10,11},{11,10},{12,13},{13,12},{17,19},{18,20},... | collective-permute-start | bytes 1572872 | tf_op jit(solution)/shard_map/ppermute | solution.py:516
  43.0 6.9 %collective-permute-start.13 = (bf16[256,1024]{1,0:T(8,128)(2,1)S(1)}, bf16[256,1024]{1,0:T(8,128)(2,1)S(1)}, u32[]{:S(2)}, u32[]{:S(2)}) collective-permute-start(bf16[256,1024]{1,0:T(8,128)(2,1)S(1)} %collective-permute-done.11.refs_5_), channel_id=1, source_target_pairs={{3,2},{5,4},{19,18},{21,20}} | collective-permute-start | bytes 1572872 | tf_op jit(solution)/shard_map/ppermute | solution.py:516
  48.6 9.9 %collective-permute-start.15 = (bf16[256,1024]{1,0:T(8,128)(2,1)S(1)}, bf16[256,1024]{1,0:T(8,128)(2,1)S(1)}, u32[]{:S(2)}, u32[]{:S(2)}) collective-permute-start(bf16[256,1024]{1,0:T(8,128)(2,1)S(1)} %collective-permute-done.8.refs_2_.refs_4_), channel_id=1, source_target_pairs={{10,12},{26,28}} | collective-permute-start | bytes 1572872 | tf_op jit(solution)/shard_map/ppermute | solution.py:516
  50.5 13.1 %collective-permute-start.14 = (bf16[256,1024]{1,0:T(8,128)(2,1)S(1)}, bf16[256,1024]{1,0:T(8,128)(2,1)S(1)}, u32[]{:S(2)}, u32[]{:S(2)}) collective-permute-start(bf16[256,1024]{1,0:T(8,128)(2,1)S(1)} %shard_map.72), channel_id=1, source_target_pairs={{1,3},{2,4},{3,5},{10,11},{11,10},{12,13},{13,12},{17,19},{18,20},... | collective-permute-start | bytes 1572872 | tf_op jit(solution)/shard_map/ppermute | solution.py:516
  66.0 8.4 %collective-permute-start.19 = (bf16[128,512]{1,0:T(8,128)(2,1)S(1)}, bf16[128,512]{1,0:T(8,128)(2,1)S(1)}, u32[]{:S(2)}, u32[]{:S(2)}) collective-permute-start(bf16[128,512]{1,0:T(8,128)(2,1)S(1)} %get-tuple-element.48), channel_id=1, source_target_pairs={{0,8},{8,0},{16,24},{24,16},{1,9},{9,1},{17,25},{25,17},{2,10},{10... | collective-permute-start | bytes 393224 | tf_op jit(solution)/shard_map/ppermute | solution.py:441
  69.9 9.2 %collective-permute-start.20 = (bf16[128,512]{1,0:T(8,128)(2,1)S(1)}, bf16[128,512]{1,0:T(8,128)(2,1)S(1)}, u32[]{:S(2)}, u32[]{:S(2)}) collective-permute-start(bf16[128,512]{1,0:T(8,128)(2,1)S(1)} %get-tuple-element.49), channel_id=1, source_target_pairs={{0,16},{8,24},{16,0},{24,8},{1,17},{9,25},{17,1},{25,9},{2,18},{10... | collective-permute-start | bytes 393224 | tf_op jit(solution)/shard_map/ppermute | solution.py:441
  70.1 9.0 %collective-permute-start.21 = (bf16[128,512]{1,0:T(8,128)(2,1)S(1)}, bf16[128,512]{1,0:T(8,128)(2,1)S(1)}, u32[]{:S(2)}, u32[]{:S(2)}) collective-permute-start(bf16[128,512]{1,0:T(8,128)(2,1)S(1)} %get-tuple-element.50), channel_id=1, source_target_pairs={{0,24},{8,16},{16,8},{24,0},{1,25},{9,17},{17,9},{25,1},{2,26},{10... | collective-permute-start | bytes 393224 | tf_op jit(solution)/shard_map/ppermute | solution.py:441
  74.0 6.5 %collective-permute-start.16 = (bf16[128,512]{1,0:T(8,128)(2,1)S(1)}, bf16[128,512]{1,0:T(8,128)(2,1)S(1)}, u32[]{:S(2)}, u32[]{:S(2)}) collective-permute-start(bf16[128,512]{1,0:T(8,128)(2,1)S(1)} %get-tuple-element.45), channel_id=1, source_target_pairs={{0,8},{8,0},{16,24},{24,16},{1,9},{9,1},{17,25},{25,17},{2,10},{10... | collective-permute-start | bytes 393224 | tf_op jit(solution)/shard_map/ppermute | solution.py:441
  74.2 6.4 %collective-permute-start.17 = (bf16[128,512]{1,0:T(8,128)(2,1)S(1)}, bf16[128,512]{1,0:T(8,128)(2,1)S(1)}, u32[]{:S(2)}, u32[]{:S(2)}) collective-permute-start(bf16[128,512]{1,0:T(8,128)(2,1)S(1)} %get-tuple-element.46), channel_id=1, source_target_pairs={{0,16},{8,24},{16,0},{24,8},{1,17},{9,25},{17,1},{25,9},{2,18},{10... | collective-permute-start | bytes 393224 | tf_op jit(solution)/shard_map/ppermute | solution.py:441
  74.4 9.1 %collective-permute-start.18 = (bf16[128,512]{1,0:T(8,128)(2,1)S(1)}, bf16[128,512]{1,0:T(8,128)(2,1)S(1)}, u32[]{:S(2)}, u32[]{:S(2)}) collective-permute-start(bf16[128,512]{1,0:T(8,128)(2,1)S(1)} %get-tuple-element.47), channel_id=1, source_target_pairs={{0,24},{8,16},{16,8},{24,0},{1,25},{9,17},{17,9},{25,1},{2,26},{10... | collective-permute-start | bytes 393224 | tf_op jit(solution)/shard_map/ppermute | solution.py:441
  (5 other events, 4.2 us)

commit v4 on v3

--- a/solution.py
+++ b/solution.py
@@ -460,7 +460,24 @@
                 )
                 column += width
         shapes = [(tokens, sum(widths))] * 2 + [(2 * tokens, sum(widths))] * (slots // 2 - 1)
-        pieces = move(place, sources, copies, shapes[: slots // 2 + 1], in_vmem, in_vmem)
+        if before:
+            pieces = move(place, sources, copies, shapes[: slots // 2 + 1], in_vmem, in_vmem)
+        else:
+            head = lax.axis_index("head")
+
+            def piece(r):
+                return jnp.concatenate(
+                    [
+                        lax.dynamic_slice_in_dim(source, (head ^ r) * width, width, 1)
+                        for source, width in zip(sources, widths)
+                    ],
+                    axis=1,
+                )
+
+            pieces = [piece(r) for r in range(min(2, slots))]
+            pieces += [
+                jnp.concatenate([piece(r), piece(r + 1)], axis=0) for r in range(2, slots, 2)
+            ]
         spots = {0: (pieces[0], 0), 1: (swap(pieces[1], 1), 0)}
         sent = pieces[2:]
         if before and sent:

time: 85.5 us -> 83.6 us (0.978)
  local copies, waits for them, and re-layouts: 5.42 us -> 1.52 us
  waiting for transfers between devices: 12.5 us -> 14.3 us
    unnamed x14 -> x8, local copies, waits for them, and re-layouts: 5.38 us -> 0.02 us
    ppermute x12, waiting for transfers between devices: 7.19 us -> 10.1 us  [swap(): return lax.ppermute(value, 'head', [(h, h ^ r) for h in range(slots)])]
    dynamic_slice x0 -> x1, local copies, waits for them, and re-layouts: none -> 1.47 us  [piece(): lax.dynamic_slice_in_dim(source, (head ^ r) * width, width, 1)]
    ppermute x10, waiting for transfers between devices: 5.28 us -> 4.21 us  [send(): held[part][k + 1] = lax.ppermute(operand, ('head', 'ctx'), pairs)]
    pallas_call x6 -> x5, Pallas kernels: 5.41 us -> 4.61 us  [move(): pl.pallas_call(kernel, out_shape=[jax.ShapeDtypeStruct(s, jnp.bfloat16) f...]
  transfers between devices with their start and end apart: 22 -> 22, of which waited for: 8 -> 6; matrix products, arithmetic and copies ran while one was open for 0% -> 0% of each run, Pallas kernels for 32% -> 33%
where the time goes in v4:
time: 83.6 us; the launch traced here: 83.1 us
  starting transfers between devices  35.2 us (42%)
  Pallas kernels  31.3 us (37%)
  waiting for transfers between devices  14.3 us (17%)
  local copies, waits for them, and re-layouts  1.52 us (2%)
    pallas_call x6, Pallas kernels, attend(): pl.pallas_call(kernel, out_shape=out_shape, in_specs=[in_smem] + [in_vmem...  24 us
    ppermute x10, starting transfers between devices, send(): held[part][k + 1] = lax.ppermute(operand, ('head', 'ctx'), pairs)  21.8 us
    ppermute x12, starting transfers between devices, swap(): return lax.ppermute(value, 'head', [(h, h ^ r) for h in range(slots)])  13.4 us
    ppermute x12, waiting for transfers between devices, swap(): return lax.ppermute(value, 'head', [(h, h ^ r) for h in range(slots)])  10.1 us
    pallas_call x5, Pallas kernels, move(): pl.pallas_call(kernel, out_shape=[jax.ShapeDtypeStruct(s, jnp.bfloat16) f...  4.61 us
    ppermute x10, waiting for transfers between devices, send(): held[part][k + 1] = lax.ppermute(operand, ('head', 'ctx'), pairs)  4.21 us
  transfers between devices with their start and end apart: 22, of which 6 were waited for; matrix products, arithmetic and copies ran while one was open for 0% of the time, Pallas kernels for 33%

profile of v4, /device:TPU:21, one launch (start us, length us, event | category | flops | bytes accessed | tf_op | source)
XLA Modules:
  0.0 83.1 jit_solution(11200100266030383172)
XLA Ops:
  0.0 1.5 %constant_dynamic-slice_fusion = (bf16[128,512]{1,0:T(8,128)(2,1)S(1)}, bf16[128,512]{1,0:T(8,128)(2,1)S(1)}, bf16[128,512]{1,0:T(8,128)(2,1)S(1)}, bf16[128,512...) fusion(bf16[128,2048]{1,0:T(8,128)(2,1)} %param.8, ...), kind=kLoop, calls=%fused_computation.3 | loop fusion | bytes 2097168 | tf_op jit(solution)/shard_map/dynamic_slice | solution.py:471
  4.1 3.1 %collective-permute-start.6 = (bf16[256,1024]{1,0:T(8,128)(2,1)S(1)}, bf16[256,1024]{1,0:T(8,128)(2,1)S(1)}, u32[]{:S(2)}, u32[]{:S(2)}) collective-permute-start(bf16[256,1024]{1,0:T(8,128)(2,1)S(1)} %shard_map.66.refs_4_), channel_id=1, source_target_pairs={{0,2},{1,3},{2,4},{3,5},{5,6},{8,9},{10,11},{12,13},{14,15},{16,18... | collective-permute-start | bytes 1572872 | tf_op jit(solution)/shard_map/ppermute | solution.py:533
  7.3 1.5 %shard_map.64.info_ref = s32[27]{0:T(128)S(1)} custom-call(s32[2]{0:T(128)S(1)} %pad_add_fusion.place_ref, s32[480]{0:T(512)S(1)} %copy-done.3, s32[4096]{0:T(1024)S(1)} %copy-done.1, s32[4,8]{1,0:T(4,128)S(1)} %bitcast.10), custom_call_target="tpu_custom_call" | custom-call | tf_op jit(solution)/shard_map/pallas_call | solution.py:142
  10.8 5.2 %collective-permute-done.1.refs_0_ = bf16[256,1024]{1,0:T(8,128)(2,1)S(1)} collective-permute-done((bf16[256,1024]{1,0:T(8,128)(2,1)S(1)}, bf16[256,1024]{1,0:T(8,128)(2,1)S(1)}, u32[]{:S(2)}, u32[]{:S(2)}) %collective-permute-start.1) | collective-permute-done | bytes 524320 | tf_op jit(solution)/shard_map/ppermute | solution.py:441
  16.9 1.7 %collective-permute-start.9 = (bf16[128,1024]{1,0:T(8,128)(2,1)S(1)}, bf16[128,1024]{1,0:T(8,128)(2,1)S(1)}, u32[]{:S(2)}, u32[]{:S(2)}) collective-permute-start(bf16[128,1024]{1,0:T(8,128)(2,1)S(1)} %slice.7), channel_id=1, source_target_pairs={{0,8},{8,0},{16,24},{24,16},{1,9},{9,1},{17,25},{25,17},{2,10},{10... | collective-permute-start | bytes 786440 | tf_op jit(solution)/shard_map/ppermute | solution.py:441
  18.7 2.1 %collective-permute-done.5.refs_0_.refs_3_.refs_6_.refs_4_ = bf16[256,1024]{1,0:T(8,128)(2,1)S(1)} collective-permute-done((bf16[256,1024]{1,0:T(8,128)(2,1)S(1)}, bf16[256,1024]{1,0:T(8,128)(2,1)S(1)}, u32[]{:S(2)}, u32[]{:S(2)}) %collective-permute-start.5) | collective-permute-done | bytes 524320 | tf_op jit(solution)/shard_map/ppermute | solution.py:533
  21.4 1.3 %collective-permute-start.12 = (bf16[256,1024]{1,0:T(8,128)(2,1)S(1)}, bf16[256,1024]{1,0:T(8,128)(2,1)S(1)}, u32[]{:S(2)}, u32[]{:S(2)}) collective-permute-start(bf16[256,1024]{1,0:T(8,128)(2,1)S(1)} %shard_map.68.refs_5_), channel_id=1, source_target_pairs={{9,12},{25,28}} | collective-permute-start | bytes 1572872 | tf_op jit(solution)/shard_map/ppermute | solution.py:533
  22.7 3.4 %collective-permute-start.11 = (bf16[256,1024]{1,0:T(8,128)(2,1)S(1)}, bf16[256,1024]{1,0:T(8,128)(2,1)S(1)}, u32[]{:S(2)}, u32[]{:S(2)}) collective-permute-start(bf16[256,1024]{1,0:T(8,128)(2,1)S(1)} %shard_map.68.refs_5_), channel_id=1, source_target_pairs={{0,2},{1,3},{2,4},{3,5},{5,6},{8,9},{10,11},{12,13},{14,15},{16,18... | collective-permute-start | bytes 1572872 | tf_op jit(solution)/shard_map/ppermute | solution.py:533
  28.6 1.7 %collective-permute-start = (bf16[128,1024]{1,0:T(8,128)(2,1)S(1)}, bf16[128,1024]{1,0:T(8,128)(2,1)S(1)}, u32[]{:S(2)}, u32[]{:S(2)}) collective-permute-start(bf16[128,1024]{1,0:T(8,128)(2,1)S(1)} %get-tuple-element.26), channel_id=1, source_target_pairs={{0,8},{8,0},{16,24},{24,16},{1,9},{9,1},{17,25},{25,17},{2,10},{10... | collective-permute-start | bytes 786440 | tf_op jit(solution)/shard_map/ppermute | solution.py:441
  31.8 2.8 %collective-permute-start.8 = (bf16[256,1024]{1,0:T(8,128)(2,1)S(1)}, bf16[256,1024]{1,0:T(8,128)(2,1)S(1)}, u32[]{:S(2)}, u32[]{:S(2)}) collective-permute-start(bf16[256,1024]{1,0:T(8,128)(2,1)S(1)} %shard_map.67), channel_id=1, source_target_pairs={{1,3},{2,4},{3,5},{10,11},{11,10},{12,13},{13,12},{17,19},{18,20},... | collective-permute-start | bytes 1572872 | tf_op jit(solution)/shard_map/ppermute | solution.py:533
  34.6 6.4 %shard_map.69 = (f32[4096,256]{1,0:T(8,128)S(1)}, f32[4096,128]{1,0:T(8,128)S(1)}) custom-call(s32[27]{0:T(128)S(1)} %shard_map.64.info_ref, s32[32,128]{1,0:T(8,128)S(1)} %bitcast.4, bf16[128,1024]{1,0:T(8,128)(2,1)S(1)} %get-tuple-element.25.refs_0_, bf16[128,1024]{1,0:T(8,128)(2,1)S(1)} %collective-permute-done.refs_1_, ...), custom_call_target="tpu_custom_call" | custom-call | flops 536870912 | bytes 2097152 | tf_op jit(solution)/shard_map/pallas_call | solution.py:382
  41.8 4.9 %shard_map.70 = (f32[4096,256]{1,0:T(8,128)S(1)}, f32[4096,128]{1,0:T(8,128)S(1)}) custom-call(s32[27]{0:T(128)S(1)} %shard_map.64.info_ref, s32[32,128]{1,0:T(8,128)S(1)} %bitcast.5, bf16[128,1024]{1,0:T(8,128)(2,1)S(1)} %get-tuple-element.25.refs_0_, ...), custom_call_target="tpu_custom_call", output_to_operand_aliasing={{0}: (10, {}), {1}: (11, {})} | custom-call | flops 1073741824 | bytes 2097152 | tf_op jit(solution)/shard_map/pallas_call | solution.py:382
  46.6 1.3 %collective-permute-start.15 = (bf16[256,1024]{1,0:T(8,128)(2,1)S(1)}, bf16[256,1024]{1,0:T(8,128)(2,1)S(1)}, u32[]{:S(2)}, u32[]{:S(2)}) collective-permute-start(bf16[256,1024]{1,0:T(8,128)(2,1)S(1)} %collective-permute-done.8.refs_2_.refs_4_), channel_id=1, source_target_pairs={{10,12},{26,28}} | collective-permute-start | bytes 1572872 | tf_op jit(solution)/shard_map/ppermute | solution.py:533
  48.5 5.9 %collective-permute-start.14 = (bf16[256,1024]{1,0:T(8,128)(2,1)S(1)}, bf16[256,1024]{1,0:T(8,128)(2,1)S(1)}, u32[]{:S(2)}, u32[]{:S(2)}) collective-permute-start(bf16[256,1024]{1,0:T(8,128)(2,1)S(1)} %shard_map.71), channel_id=1, source_target_pairs={{1,3},{2,4},{3,5},{10,11},{11,10},{12,13},{13,12},{17,19},{18,20},... | collective-permute-start | bytes 1572872 | tf_op jit(solution)/shard_map/ppermute | solution.py:533
  54.5 2.1 %collective-permute-done.15.refs_8_ = bf16[256,1024]{1,0:T(8,128)(2,1)S(1)} collective-permute-done((bf16[256,1024]{1,0:T(8,128)(2,1)S(1)}, bf16[256,1024]{1,0:T(8,128)(2,1)S(1)}, u32[]{:S(2)}, u32[]{:S(2)}) %collective-permute-start.15) | collective-permute-done | bytes 524320 | tf_op jit(solution)/shard_map/ppermute | solution.py:533
  56.6 5.0 %shard_map.72 = (f32[4096,256]{1,0:T(8,128)S(1)}, f32[4096,128]{1,0:T(8,128)S(1)}) custom-call(s32[27]{0:T(128)S(1)} %shard_map.64.info_ref, s32[32,128]{1,0:T(8,128)S(1)} %bitcast.6, bf16[128,1024]{1,0:T(8,128)(2,1)S(1)} %get-tuple-element.25.refs_0_, ...), custom_call_target="tpu_custom_call", output_to_operand_aliasing={{0}: (12, {}), {1}: (13, {})} | custom-call | flops 1610612736 | bytes 2097152 | tf_op jit(solution)/shard_map/pallas_call | solution.py:382
  61.6 2.4 %shard_map.74 = (bf16[128,512]{1,0:T(8,128)(2,1)S(1)}, bf16[128,512]{1,0:T(8,128)(2,1)S(1)}, bf16[128,512]{1,0:T(8,128)(2,1)S(1)}) custom-call(s32[27]{0:T(128)S(1)} %shard_map.64.info_ref, s32[32,128]{1,0:T(8,128)S(1)} %bitcast.7, bf16[128,1024]{1,0:T(8,128)(2,1)S(1)} %get-tuple-element.25.refs_0_, bf16[128,1024]{1,0:T(8,128)(2,1)S(1)} %collective-permute-done.refs_1_, ...), custom_call_target="tpu_custom_call" | custom-call | flops 268435456 | bytes 2097152 | tf_op jit(solution)/shard_map/pallas_call | solution.py:382
  64.0 3.9 %collective-permute-start.19 = (bf16[128,512]{1,0:T(8,128)(2,1)S(1)}, bf16[128,512]{1,0:T(8,128)(2,1)S(1)}, u32[]{:S(2)}, u32[]{:S(2)}) collective-permute-start(bf16[128,512]{1,0:T(8,128)(2,1)S(1)} %get-tuple-element.42), channel_id=1, source_target_pairs={{0,8},{8,0},{16,24},{24,16},{1,9},{9,1},{17,25},{25,17},{2,10},{10... | collective-permute-start | bytes 393224 | tf_op jit(solution)/shard_map/ppermute | solution.py:441
  69.7 2.4 %shard_map.73 = (bf16[128,512]{1,0:T(8,128)(2,1)S(1)}, bf16[128,512]{1,0:T(8,128)(2,1)S(1)}, bf16[128,512]{1,0:T(8,128)(2,1)S(1)}) custom-call(s32[27]{0:T(128)S(1)} %shard_map.64.info_ref, s32[32,128]{1,0:T(8,128)S(1)} %bitcast.8, bf16[128,1024]{1,0:T(8,128)(2,1)S(1)} %get-tuple-element.25.refs_0_, bf16[128,1024]{1,0:T(8,128)(2,1)S(1)} %collective-permute-done.refs_1_, ...), custom_call_target="tpu_custom_call" | custom-call | flops 268435456 | bytes 2097152 | tf_op jit(solution)/shard_map/pallas_call | solution.py:382
  72.8 1.5 %collective-permute-start.18 = (bf16[128,512]{1,0:T(8,128)(2,1)S(1)}, bf16[128,512]{1,0:T(8,128)(2,1)S(1)}, u32[]{:S(2)}, u32[]{:S(2)}) collective-permute-start(bf16[128,512]{1,0:T(8,128)(2,1)S(1)} %get-tuple-element.41), channel_id=1, source_target_pairs={{0,24},{8,16},{16,8},{24,0},{1,25},{9,17},{17,9},{25,1},{2,26},{10... | collective-permute-start | bytes 393224 | tf_op jit(solution)/shard_map/ppermute | solution.py:441
  74.3 2.9 %shard_map.75.refs_3_ = bf16[128,1024]{1,0:T(8,128)(2,1)S(1)} custom-call(s32[27]{0:T(128)S(1)} %shard_map.64.info_ref, s32[32,128]{1,0:T(8,128)S(1)} %bitcast.9, bf16[128,1024]{1,0:T(8,128)(2,1)S(1)} %get-tuple-element.25.refs_0_, bf16[128,1024]{1,0:T(8,128)(2,1)S(1)} %collective-permute-done.refs_1_, bf16[256,1024]{1,0:T(8,128)(2,1)S(1)} %collective-permute-done.2.refs_2_, ...), custom_call_target="tpu_custom_call" | custom-call | flops 536870912 | bytes 2097152 | tf_op jit(solution)/shard_map/pallas_call | solution.py:382
  77.2 1.4 %shard_map.76.refs_3_ = bf16[128,4096]{1,0:T(8,128)(2,1)} custom-call(s32[2]{0:T(128)S(1)} %pad_add_fusion.place_ref, bf16[128,512]{1,0:T(8,128)(2,1)S(1)} %collective-permute-done.19.refs_0_, bf16[128,512]{1,0:T(8,128)(2,1)S(1)} %collective-permute-done.20.refs_1_, bf16[128,512]{1,0:T(8,128)(2,1)S(1)} %collective-permute-done.21.refs_2_, ...), custom_call_target="tpu_custom_call" | custom-call | bytes 1310720 | tf_op jit(solution)/shard_map/pallas_call | solution.py:100
  78.7 3.0 %collective-permute-done.18.refs_2_ = bf16[128,512]{1,0:T(8,128)(2,1)S(1)} collective-permute-done((bf16[128,512]{1,0:T(8,128)(2,1)S(1)}, bf16[128,512]{1,0:T(8,128)(2,1)S(1)}, u32[]{:S(2)}, u32[]{:S(2)}) %collective-permute-start.18) | collective-permute-done | bytes 131104 | tf_op jit(solution)/shard_map/ppermute | solution.py:441
  81.6 1.3 %shard_map.77 = bf16[128,4096]{1,0:T(8,128)(2,1)} custom-call(s32[2]{0:T(128)S(1)} %pad_add_fusion.place_ref, bf16[128,512]{1,0:T(8,128)(2,1)S(1)} %collective-permute-done.16.refs_0_, bf16[128,512]{1,0:T(8,128)(2,1)S(1)} %collective-permute-done.17.refs_1_, bf16[128,512]{1,0:T(8,128)(2,1)S(1)} %collective-permute-done.18.refs_2_, ...), custom_call_target="tpu_custom_call", output_to_operand_aliasing={{}: (4, {})} | custom-call | bytes 786432 | tf_op jit(solution)/shard_map/pallas_call | solution.py:100
  (49 shorter events, 13.8 us)
Async XLA Ops:
  0.0 7.2 %copy-start.2 = (s32[8,4]{0,1:T(4,128)S(1)}, s32[8,4]{0,1:T(4,128)}, u32[]{:S(2)}) copy-start(s32[8,4]{0,1:T(4,128)} %param.10) | copy-start | bytes 388
  0.0 10.1 %copy-start = (bf16[128,4096]{1,0:T(8,128)(2,1)S(1)}, bf16[128,4096]{1,0:T(8,128)(2,1)}, u32[]{:S(2)}) copy-start(bf16[128,4096]{1,0:T(8,128)(2,1)} %refs_0_.1) | copy-start | bytes 3145732
  1.5 1.9 %collective-permute-start.4 = (bf16[128,1024]{1,0:T(8,128)(2,1)S(1)}, bf16[128,1024]{1,0:T(8,128)(2,1)S(1)}, u32[]{:S(2)}, u32[]{:S(2)}) collective-permute-start(bf16[128,1024]{1,0:T(8,128)(2,1)S(1)} %pad_maximum_fusion.1), channel_id=1, source_target_pairs={{0,8},{8,0},{16,24},{24,16},{1,9},{9,1},{17,25},{25,17},{2,10},{10... | collective-permute-start | bytes 786440 | tf_op jit(solution)/shard_map/ppermute | solution.py:441
  2.4 13.6 %collective-permute-start.1 = (bf16[256,1024]{1,0:T(8,128)(2,1)S(1)}, bf16[256,1024]{1,0:T(8,128)(2,1)S(1)}, u32[]{:S(2)}, u32[]{:S(2)}) collective-permute-start(bf16[256,1024]{1,0:T(8,128)(2,1)S(1)} %maximum_maximum_fusion), channel_id=1, source_target_pairs={{0,16},{8,24},{16,0},{24,8},{1,17},{9,25},{17,1},{25,9},{2,18},{10... | collective-permute-start | bytes 1572872 | tf_op jit(solution)/shard_map/ppermute | solution.py:441
  4.1 12.1 %collective-permute-start.6 = (bf16[256,1024]{1,0:T(8,128)(2,1)S(1)}, bf16[256,1024]{1,0:T(8,128)(2,1)S(1)}, u32[]{:S(2)}, u32[]{:S(2)}) collective-permute-start(bf16[256,1024]{1,0:T(8,128)(2,1)S(1)} %shard_map.66.refs_4_), channel_id=1, source_target_pairs={{0,2},{1,3},{2,4},{3,5},{5,6},{8,9},{10,11},{12,13},{14,15},{16,18... | collective-permute-start | bytes 1572872 | tf_op jit(solution)/shard_map/ppermute | solution.py:533
  8.8 12.0 %collective-permute-start.5 = (bf16[256,1024]{1,0:T(8,128)(2,1)S(1)}, bf16[256,1024]{1,0:T(8,128)(2,1)S(1)}, u32[]{:S(2)}, u32[]{:S(2)}) collective-permute-start(bf16[256,1024]{1,0:T(8,128)(2,1)S(1)} %shard_map.66.refs_4_), channel_id=1, source_target_pairs={{0,1},{2,3},{4,5},{6,7},{8,10},{9,11},{10,12},{11,13},{13,14},{16,... | collective-permute-start | bytes 1572872 | tf_op jit(solution)/shard_map/ppermute | solution.py:533
  16.0 12.7 %collective-permute-start.2 = (bf16[256,1024]{1,0:T(8,128)(2,1)S(1)}, bf16[256,1024]{1,0:T(8,128)(2,1)S(1)}, u32[]{:S(2)}, u32[]{:S(2)}) collective-permute-start(bf16[256,1024]{1,0:T(8,128)(2,1)S(1)} %get-tuple-element.28), channel_id=1, source_target_pairs={{0,16},{8,24},{16,0},{24,8},{1,17},{9,25},{17,1},{25,9},{2,18},{10... | collective-permute-start | bytes 1572872 | tf_op jit(solution)/shard_map/ppermute | solution.py:441
  16.2 14.1 %collective-permute-start.7 = (bf16[256,1024]{1,0:T(8,128)(2,1)S(1)}, bf16[256,1024]{1,0:T(8,128)(2,1)S(1)}, u32[]{:S(2)}, u32[]{:S(2)}) collective-permute-start(bf16[256,1024]{1,0:T(8,128)(2,1)S(1)} %collective-permute-done.6.refs_2_.refs_4_), channel_id=1, source_target_pairs={{3,2},{5,4},{19,18},{21,20}} | collective-permute-start | bytes 1572872 | tf_op jit(solution)/shard_map/ppermute | solution.py:533
  16.9 3.8 %collective-permute-start.9 = (bf16[128,1024]{1,0:T(8,128)(2,1)S(1)}, bf16[128,1024]{1,0:T(8,128)(2,1)S(1)}, u32[]{:S(2)}, u32[]{:S(2)}) collective-permute-start(bf16[128,1024]{1,0:T(8,128)(2,1)S(1)} %slice.7), channel_id=1, source_target_pairs={{0,8},{8,0},{16,24},{24,16},{1,9},{9,1},{17,25},{25,17},{2,10},{10... | collective-permute-start | bytes 786440 | tf_op jit(solution)/shard_map/ppermute | solution.py:441
  21.4 19.7 %collective-permute-start.12 = (bf16[256,1024]{1,0:T(8,128)(2,1)S(1)}, bf16[256,1024]{1,0:T(8,128)(2,1)S(1)}, u32[]{:S(2)}, u32[]{:S(2)}) collective-permute-start(bf16[256,1024]{1,0:T(8,128)(2,1)S(1)} %shard_map.68.refs_5_), channel_id=1, source_target_pairs={{9,12},{25,28}} | collective-permute-start | bytes 1572872 | tf_op jit(solution)/shard_map/ppermute | solution.py:533
  22.7 18.4 %collective-permute-start.11 = (bf16[256,1024]{1,0:T(8,128)(2,1)S(1)}, bf16[256,1024]{1,0:T(8,128)(2,1)S(1)}, u32[]{:S(2)}, u32[]{:S(2)}) collective-permute-start(bf16[256,1024]{1,0:T(8,128)(2,1)S(1)} %shard_map.68.refs_5_), channel_id=1, source_target_pairs={{0,2},{1,3},{2,4},{3,5},{5,6},{8,9},{10,11},{12,13},{14,15},{16,18... | collective-permute-start | bytes 1572872 | tf_op jit(solution)/shard_map/ppermute | solution.py:533
  26.1 15.0 %collective-permute-start.10 = (bf16[256,1024]{1,0:T(8,128)(2,1)S(1)}, bf16[256,1024]{1,0:T(8,128)(2,1)S(1)}, u32[]{:S(2)}, u32[]{:S(2)}) collective-permute-start(bf16[256,1024]{1,0:T(8,128)(2,1)S(1)} %shard_map.68.refs_5_), channel_id=1, source_target_pairs={{0,1},{2,3},{4,5},{6,7},{8,10},{9,11},{10,12},{11,13},{13,14},{16,... | collective-permute-start | bytes 1572872 | tf_op jit(solution)/shard_map/ppermute | solution.py:533
  28.6 3.2 %collective-permute-start = (bf16[128,1024]{1,0:T(8,128)(2,1)S(1)}, bf16[128,1024]{1,0:T(8,128)(2,1)S(1)}, u32[]{:S(2)}, u32[]{:S(2)}) collective-permute-start(bf16[128,1024]{1,0:T(8,128)(2,1)S(1)} %get-tuple-element.26), channel_id=1, source_target_pairs={{0,8},{8,0},{16,24},{24,16},{1,9},{9,1},{17,25},{25,17},{2,10},{10... | collective-permute-start | bytes 786440 | tf_op jit(solution)/shard_map/ppermute | solution.py:441
  30.3 4.2 %collective-permute-start.3 = (bf16[128,1024]{1,0:T(8,128)(2,1)S(1)}, bf16[128,1024]{1,0:T(8,128)(2,1)S(1)}, u32[]{:S(2)}, u32[]{:S(2)}) collective-permute-start(bf16[128,1024]{1,0:T(8,128)(2,1)S(1)} %slice.8), channel_id=1, source_target_pairs={{0,8},{8,0},{16,24},{24,16},{1,9},{9,1},{17,25},{25,17},{2,10},{10... | collective-permute-start | bytes 786440 | tf_op jit(solution)/shard_map/ppermute | solution.py:441
  31.8 14.8 %collective-permute-start.8 = (bf16[256,1024]{1,0:T(8,128)(2,1)S(1)}, bf16[256,1024]{1,0:T(8,128)(2,1)S(1)}, u32[]{:S(2)}, u32[]{:S(2)}) collective-permute-start(bf16[256,1024]{1,0:T(8,128)(2,1)S(1)} %shard_map.67), channel_id=1, source_target_pairs={{1,3},{2,4},{3,5},{10,11},{11,10},{12,13},{13,12},{17,19},{18,20},... | collective-permute-start | bytes 1572872 | tf_op jit(solution)/shard_map/ppermute | solution.py:533
  41.1 6.9 %collective-permute-start.13 = (bf16[256,1024]{1,0:T(8,128)(2,1)S(1)}, bf16[256,1024]{1,0:T(8,128)(2,1)S(1)}, u32[]{:S(2)}, u32[]{:S(2)}) collective-permute-start(bf16[256,1024]{1,0:T(8,128)(2,1)S(1)} %collective-permute-done.11.refs_5_), channel_id=1, source_target_pairs={{3,2},{5,4},{19,18},{21,20}} | collective-permute-start | bytes 1572872 | tf_op jit(solution)/shard_map/ppermute | solution.py:533
  46.6 9.9 %collective-permute-start.15 = (bf16[256,1024]{1,0:T(8,128)(2,1)S(1)}, bf16[256,1024]{1,0:T(8,128)(2,1)S(1)}, u32[]{:S(2)}, u32[]{:S(2)}) collective-permute-start(bf16[256,1024]{1,0:T(8,128)(2,1)S(1)} %collective-permute-done.8.refs_2_.refs_4_), channel_id=1, source_target_pairs={{10,12},{26,28}} | collective-permute-start | bytes 1572872 | tf_op jit(solution)/shard_map/ppermute | solution.py:533
  48.5 13.1 %collective-permute-start.14 = (bf16[256,1024]{1,0:T(8,128)(2,1)S(1)}, bf16[256,1024]{1,0:T(8,128)(2,1)S(1)}, u32[]{:S(2)}, u32[]{:S(2)}) collective-permute-start(bf16[256,1024]{1,0:T(8,128)(2,1)S(1)} %shard_map.71), channel_id=1, source_target_pairs={{1,3},{2,4},{3,5},{10,11},{11,10},{12,13},{13,12},{17,19},{18,20},... | collective-permute-start | bytes 1572872 | tf_op jit(solution)/shard_map/ppermute | solution.py:533
  64.0 8.7 %collective-permute-start.19 = (bf16[128,512]{1,0:T(8,128)(2,1)S(1)}, bf16[128,512]{1,0:T(8,128)(2,1)S(1)}, u32[]{:S(2)}, u32[]{:S(2)}) collective-permute-start(bf16[128,512]{1,0:T(8,128)(2,1)S(1)} %get-tuple-element.42), channel_id=1, source_target_pairs={{0,8},{8,0},{16,24},{24,16},{1,9},{9,1},{17,25},{25,17},{2,10},{10... | collective-permute-start | bytes 393224 | tf_op jit(solution)/shard_map/ppermute | solution.py:441
  68.0 9.2 %collective-permute-start.20 = (bf16[128,512]{1,0:T(8,128)(2,1)S(1)}, bf16[128,512]{1,0:T(8,128)(2,1)S(1)}, u32[]{:S(2)}, u32[]{:S(2)}) collective-permute-start(bf16[128,512]{1,0:T(8,128)(2,1)S(1)} %get-tuple-element.43), channel_id=1, source_target_pairs={{0,16},{8,24},{16,0},{24,8},{1,17},{9,25},{17,1},{25,9},{2,18},{10... | collective-permute-start | bytes 393224 | tf_op jit(solution)/shard_map/ppermute | solution.py:441
  68.4 8.7 %collective-permute-start.21 = (bf16[128,512]{1,0:T(8,128)(2,1)S(1)}, bf16[128,512]{1,0:T(8,128)(2,1)S(1)}, u32[]{:S(2)}, u32[]{:S(2)}) collective-permute-start(bf16[128,512]{1,0:T(8,128)(2,1)S(1)} %get-tuple-element.44), channel_id=1, source_target_pairs={{0,24},{8,16},{16,8},{24,0},{1,25},{9,17},{17,9},{25,1},{2,26},{10... | collective-permute-start | bytes 393224 | tf_op jit(solution)/shard_map/ppermute | solution.py:441
  72.1 6.5 %collective-permute-start.16 = (bf16[128,512]{1,0:T(8,128)(2,1)S(1)}, bf16[128,512]{1,0:T(8,128)(2,1)S(1)}, u32[]{:S(2)}, u32[]{:S(2)}) collective-permute-start(bf16[128,512]{1,0:T(8,128)(2,1)S(1)} %get-tuple-element.39), channel_id=1, source_target_pairs={{0,8},{8,0},{16,24},{24,16},{1,9},{9,1},{17,25},{25,17},{2,10},{10... | collective-permute-start | bytes 393224 | tf_op jit(solution)/shard_map/ppermute | solution.py:441
  72.3 6.4 %collective-permute-start.17 = (bf16[128,512]{1,0:T(8,128)(2,1)S(1)}, bf16[128,512]{1,0:T(8,128)(2,1)S(1)}, u32[]{:S(2)}, u32[]{:S(2)}) collective-permute-start(bf16[128,512]{1,0:T(8,128)(2,1)S(1)} %get-tuple-element.40), channel_id=1, source_target_pairs={{0,16},{8,24},{16,0},{24,8},{1,17},{9,25},{17,1},{25,9},{2,18},{10... | collective-permute-start | bytes 393224 | tf_op jit(solution)/shard_map/ppermute | solution.py:441
  72.8 8.9 %collective-permute-start.18 = (bf16[128,512]{1,0:T(8,128)(2,1)S(1)}, bf16[128,512]{1,0:T(8,128)(2,1)S(1)}, u32[]{:S(2)}, u32[]{:S(2)}) collective-permute-start(bf16[128,512]{1,0:T(8,128)(2,1)S(1)} %get-tuple-element.41), channel_id=1, source_target_pairs={{0,24},{8,16},{16,8},{24,0},{1,25},{9,17},{17,9},{25,1},{2,26},{10... | collective-permute-start | bytes 393224 | tf_op jit(solution)/shard_map/ppermute | solution.py:441
  (2 other events, 14.5 us)
